TPU v7x, 32 devices: a whole 2x2x4 slice. The times are simulated.
32 devices in a mesh: batch: 8 (over z, y), seq: 4 (over x, core).
Axes of the slice: x: 2, y: 2, z: 4, core: 2. Of those that a mesh axis runs over, the one named last changes fastest.
Arguments:
- tokens: bfloat16 [8192, 1024], P(('batch', 'seq')), may hold values from -6 to 6
- cotangent: bfloat16 [8192, 1024], P(('batch', 'seq')), may hold values from -6 to 6
- w_project: float32 [1024, 4120], P(('batch', 'seq')), may hold values from -0.1875 to 0.1875
- w_mixout: float32 [2048, 1024], P(('batch', 'seq')), may hold values from -0.125 to 0.125
- w_gateup: float32 [1024, 4096], P(('batch', 'seq')), may hold values from -0.1875 to 0.1875
- w_down: float32 [2048, 1024], P(('batch', 'seq')), may hold values from -0.125 to 0.125
- gains: float32 [3584], P(('batch', 'seq')), may hold values from 0.5 to 1.5
- conv_params: float32 [5, 1792], P(None, ('batch', 'seq')), may hold values from -3 to 3
- head_params: float32 [3, 24], replicated, may hold values from -8 to 1.5
- mom_project: float32 [1024, 4120], P(('batch', 'seq')), may hold values from -32 to 32
- sec_project: float32 [1024, 4120], P(('batch', 'seq')), may hold values from 106.496 to 434.176
- mom_mixout: float32 [2048, 1024], P(('batch', 'seq')), may hold values from -32 to 32
- sec_mixout: float32 [2048, 1024], P(('batch', 'seq')), may hold values from 106.496 to 434.176
- mom_gateup: float32 [1024, 4096], P(('batch', 'seq')), may hold values from -32 to 32
- sec_gateup: float32 [1024, 4096], P(('batch', 'seq')), may hold values from 106.496 to 434.176
- mom_down: float32 [2048, 1024], P(('batch', 'seq')), may hold values from -32 to 32
- sec_down: float32 [2048, 1024], P(('batch', 'seq')), may hold values from 106.496 to 434.176
- mom_gains: float32 [3584], P(('batch', 'seq')), may hold values from -64 to 64
- sec_gains: float32 [3584], P(('batch', 'seq')), may hold values from 434.176 to 1720.32
- mom_conv: float32 [5, 1792], P(None, ('batch', 'seq')), may hold values from -64 to 64
- sec_conv: float32 [5, 1792], P(None, ('batch', 'seq')), may hold values from 434.176 to 1720.32
- mom_head: float32 [3, 24], replicated, may hold values from -192 to 192
- sec_head: float32 [3, 24], replicated, may hold values from 4096 to 16384
Outputs:
- out_block: bfloat16 [8192, 1024], P(('batch', 'seq'))
- grad_tokens: float32 [8192, 1024], P(('batch', 'seq'))
- next_mom_project: float32 [1024, 4120], P(('batch', 'seq'))
- next_sec_project: float32 [1024, 4120], P(('batch', 'seq'))
- next_w_project: float32 [1024, 4120], P(('batch', 'seq'))
- next_mom_mixout: float32 [2048, 1024], P(('batch', 'seq'))
- next_sec_mixout: float32 [2048, 1024], P(('batch', 'seq'))
- next_w_mixout: float32 [2048, 1024], P(('batch', 'seq'))
- next_mom_gateup: float32 [1024, 4096], P(('batch', 'seq'))
- next_sec_gateup: float32 [1024, 4096], P(('batch', 'seq'))
- next_w_gateup: float32 [1024, 4096], P(('batch', 'seq'))
- next_mom_down: float32 [2048, 1024], P(('batch', 'seq'))
- next_sec_down: float32 [2048, 1024], P(('batch', 'seq'))
- next_w_down: float32 [2048, 1024], P(('batch', 'seq'))
- next_mom_gains: float32 [3584], P(('batch', 'seq'))
- next_sec_gains: float32 [3584], P(('batch', 'seq'))
- next_w_gains: float32 [3584], P(('batch', 'seq'))
- next_mom_conv: float32 [5, 1792], P(None, ('batch', 'seq'))
- next_sec_conv: float32 [5, 1792], P(None, ('batch', 'seq'))
- next_w_conv: float32 [5, 1792], P(None, ('batch', 'seq'))
- next_mom_head: float32 [3, 24], replicated
- next_sec_head: float32 [3, 24], replicated
- next_w_head: float32 [3, 24], replicated
All inputs are finite; a program needn't handle non-finite values.
Results may differ from a plain program's by a relative error of at most 0.015.
The roundings to bfloat16 on the way count: a program that leaves them out, or rounds other values in their place, can miss the bound.
Values may be sent and summed in bfloat16 or wider, within the bound.
A program may use at most 192 MiB of HBM per device.

v0:
```python
import jax
import jax.numpy as jnp
from jax import lax
from jax.sharding import PartitionSpec as P

D = 1024
FF = 2048
HEADS = 8
KV_HEADS = 2
HEAD_DIM = 64
M_HEADS = 24
M_DIM = 64
STATE = 128
CONV = 4
STEP = 10


epsilon = 1e-05
rope_base = 100000000000.0
beta_one = 0.9
beta_two = 0.95
adam_eps = 1e-08
weight_decay = 0.1
rate_matrix = 0.06
rate_vector = 1.0
highest = lax.Precision.HIGHEST


def from_behind(value, axis, by):
    length = lax.axis_size(axis)
    pairs = [(i, i + by) for i in range(length) if 0 <= i + by < length]
    return lax.ppermute(value, axis, pairs)


def entering(value, axis, join, neutral):
    place = lax.axis_index(axis)
    gathered = jax.tree.map(
        lambda a, kind: lax.all_gather(a.astype(kind), axis), value, (jnp.bfloat16, jnp.bfloat16)
    )
    state = jax.tree.map(lambda a, e: jnp.zeros_like(a) + jnp.asarray(e, a.dtype), value, neutral)

    def one(turn, state):
        return join(
            state,
            jax.tree.map(
                lambda a, own: lax.dynamic_index_in_dim(a, turn, 0, False).astype(own.dtype),
                gathered,
                value,
            ),
        )

    return lax.fori_loop(0, place, one, state)


def entering_2(value, axis, combine, identity):
    length, index = (lax.axis_size(axis), lax.axis_index(axis))
    everything = jax.tree.map(
        lambda part, kind: lax.all_gather(part.astype(kind), axis),
        value,
        jax.tree.map(lambda a: jnp.bfloat16 if a.dtype == jnp.float32 else a.dtype, value),
    )
    start = jax.tree.map(
        lambda part, zero: jnp.broadcast_to(jnp.asarray(zero, part.dtype), part.shape),
        value,
        identity,
    )

    def turn(k, before):
        at = length - 1 - k
        reached = at > index
        new = combine(
            before, jax.tree.map(lambda part, own: part[at].astype(own.dtype), everything, value)
        )
        return jax.tree.map(lambda a, b: jnp.where(reached, a, b), new, before)

    return lax.fori_loop(0, length, turn, start)


def hp_matmul(left, right):
    return jnp.dot(left, right, precision=highest, preferred_element_type=jnp.float32)


def rms_scale(values, gain_vector):
    return (
        values
        * lax.rsqrt(jnp.mean(values * values, axis=-1, keepdims=True) + epsilon)
        * gain_vector
    )


def rope_tables(positions):
    half_dim = HEAD_DIM // 2
    frequency = jnp.power(rope_base, -2.0 * jnp.arange(half_dim, dtype=jnp.float32) / HEAD_DIM)
    angles = positions.astype(jnp.float32)[:, None] * frequency[None, :]
    return (jnp.cos(angles)[:, None, :], jnp.sin(angles)[:, None, :])


def rotate(heads, cosine, sine_table):
    half_dim = HEAD_DIM // 2
    first_half = heads[..., :half_dim]
    second_half = heads[..., half_dim:]
    return jnp.concatenate(
        [
            first_half * cosine - second_half * sine_table,
            second_half * cosine + first_half * sine_table,
        ],
        axis=-1,
    )


def prepare(padded, conv_taps, head_params, dt_raw):
    row_count = dt_raw.shape[0]
    inner_width = M_HEADS * M_DIM
    summed = conv_taps[CONV]
    for tap_index in range(CONV):
        summed = summed + conv_taps[tap_index] * padded[tap_index : tap_index + row_count]
    activated = jax.nn.silu(summed)
    x_heads = activated[:, :inner_width].reshape(row_count, M_HEADS, M_DIM)
    b_matrix = activated[:, inner_width : inner_width + STATE]
    c_matrix = activated[:, inner_width + STATE :]
    step_size = jax.nn.softplus(dt_raw + head_params[0])
    log_decay = -step_size * jnp.exp(head_params[1])
    return (step_size[:, :, None] * x_heads, log_decay, b_matrix, c_matrix, x_heads)


def local_state(inputs, log_decay, b_matrix):
    cumulated = jnp.cumsum(log_decay, axis=0)
    tail_decay = jnp.exp(cumulated[-1][None, :] - cumulated)
    end_state = jnp.einsum(
        "shp,sn->hpn", tail_decay[:, :, None] * inputs, b_matrix, precision=highest
    )
    return (jnp.exp(cumulated[-1]), end_state)


def mamba_output(
    inputs, log_decay, b_matrix, c_matrix, x_heads, gate_z, head_params, gain_vector, start_state
):
    row_count = log_decay.shape[0]
    cumulated = jnp.cumsum(log_decay, axis=0)
    lower_mask = (jnp.arange(row_count)[:, None] >= jnp.arange(row_count)[None, :])[:, :, None]
    log_gaps = jnp.where(lower_mask, cumulated[:, None, :] - cumulated[None, :, :], -1e30)
    mixing = hp_matmul(c_matrix, b_matrix.T)[:, :, None] * jnp.exp(log_gaps)
    within = jnp.einsum("tsh,shp->thp", mixing, inputs, precision=highest)
    carried = (
        jnp.einsum("tn,hpn->thp", c_matrix, start_state, precision=highest)
        * jnp.exp(cumulated)[:, :, None]
    )
    output = within + carried + head_params[2][None, :, None] * x_heads
    gated = output.reshape(row_count, M_HEADS * M_DIM) * jax.nn.silu(gate_z)
    return rms_scale(gated, gain_vector)


def chain_step(earlier, later):
    return (earlier[0] * later[0], later[0][:, None, None] * earlier[1] + later[1])


def swiglu(gate_up):
    return jax.nn.silu(gate_up[:, :FF]) * gate_up[:, FF:]


def adamw_update(weight, gradient, moment_one, moment_two, rate, decay):
    moment_one = beta_one * moment_one + (1.0 - beta_one) * gradient
    moment_two = beta_two * moment_two + (1.0 - beta_two) * gradient * gradient
    corrected_one = moment_one / (1.0 - beta_one**STEP)
    corrected_two = moment_two / (1.0 - beta_two**STEP)
    new_weight = weight - rate * (
        corrected_one / (jnp.sqrt(corrected_two) + adam_eps) + decay * weight
    )
    return (moment_one, moment_two, new_weight)


def local(
    tokens,
    cotangent,
    w_project,
    w_mixout,
    w_gateup,
    w_down,
    gains,
    conv_params,
    head_params,
    mom_project,
    sec_project,
    mom_mixout,
    sec_mixout,
    mom_gateup,
    sec_gateup,
    mom_down,
    sec_down,
    mom_gains,
    sec_gains,
    mom_conv,
    sec_conv,
    mom_head,
    sec_head,
):
    row_count = tokens.shape[0]
    group_size = HEADS // KV_HEADS
    scale_factor = HEAD_DIM ** (-0.5)
    q_width = HEADS * HEAD_DIM
    kv_width = KV_HEADS * HEAD_DIM
    inner_width = M_HEADS * M_DIM
    conv_width = inner_width + 2 * STATE
    offset_cols = q_width + 2 * kv_width
    out_multiplier = (row_count * lax.axis_size("seq") / 6.0) ** 0.5
    full_project, full_mixout, full_gateup, full_down, full_gains, full_conv = (
        lax.all_gather(w_project.astype(jnp.bfloat16), ("batch", "seq"), axis=0, tiled=True),
        lax.all_gather(w_mixout.astype(jnp.bfloat16), ("batch", "seq"), axis=0, tiled=True),
        lax.all_gather(w_gateup.astype(jnp.bfloat16), ("batch", "seq"), axis=0, tiled=True),
        lax.all_gather(w_down.astype(jnp.bfloat16), ("batch", "seq"), axis=0, tiled=True),
        lax.all_gather(gains.astype(jnp.bfloat16), ("batch", "seq"), axis=0, tiled=True),
        lax.all_gather(conv_params.astype(jnp.bfloat16), ("batch", "seq"), axis=1, tiled=True),
    )
    gains_f = full_gains.astype(jnp.float32)
    gain_first = gains_f[:D]
    gain_second = gains_f[D : 2 * D]
    gain_mamba = gains_f[2 * D :]
    conv_taps = full_conv.astype(jnp.float32)
    tokens_f = tokens.astype(jnp.float32)
    normed_f, pull_first = jax.vjp(rms_scale, tokens_f, gain_first)
    normed = normed_f.astype(jnp.bfloat16)
    projected = jnp.dot(normed, full_project, preferred_element_type=jnp.float32)
    seq_index = lax.axis_index("seq")
    positions = seq_index * row_count + jnp.arange(row_count, dtype=jnp.int32)
    cosine, sine_table = rope_tables(positions)

    def rope_pair(query_part, key_part):
        return (
            rotate(query_part.reshape(row_count, HEADS, HEAD_DIM), cosine, sine_table),
            rotate(key_part.reshape(row_count, KV_HEADS, HEAD_DIM), cosine, sine_table),
        )

    (query_rot, key_rot), pull_rope = jax.vjp(
        rope_pair, projected[:, :q_width], projected[:, q_width : q_width + kv_width]
    )
    queries = query_rot.astype(jnp.bfloat16).reshape(row_count, KV_HEADS, group_size, HEAD_DIM)
    key_local = key_rot.reshape(row_count, kv_width).astype(jnp.bfloat16)
    value_local = projected[:, q_width + kv_width : offset_cols].astype(jnp.bfloat16)
    key_all, value_all = (
        lax.all_gather(key_local, "seq", axis=0, tiled=True),
        lax.all_gather(value_local, "seq", axis=0, tiled=True),
    )

    def scores_for(key_source, shard):
        key_block = lax.dynamic_slice_in_dim(key_source, shard * row_count, row_count, 0)
        key_block = key_block.reshape(row_count, KV_HEADS, HEAD_DIM)
        raw_scores = (
            jnp.einsum("qkgd,skd->kgqs", queries, key_block, preferred_element_type=jnp.float32)
            * scale_factor
        )
        key_pos = shard * row_count + jnp.arange(row_count, dtype=jnp.int32)
        allowed = key_pos[None, :] <= positions[:, None]
        return jnp.where(allowed, raw_scores, -1e30)

    def value_block(value_source, shard):
        picked = lax.dynamic_slice_in_dim(value_source, shard * row_count, row_count, 0)
        return picked.reshape(row_count, KV_HEADS, HEAD_DIM)

    def max_step(shard, carry):
        row_top, row_total = carry
        scores = scores_for(key_all, shard)
        new_top = jnp.maximum(row_top, jnp.max(scores, axis=-1))
        row_total = row_total * jnp.exp(row_top - new_top) + jnp.sum(
            jnp.exp(scores - new_top[..., None]), axis=-1
        )
        return (new_top, row_total)

    start_top = jnp.full((KV_HEADS, group_size, row_count), -1e30, jnp.float32)
    row_top, row_total = lax.fori_loop(
        0, seq_index + 1, max_step, (start_top, jnp.zeros_like(start_top))
    )
    log_total = row_top + jnp.log(row_total)

    def out_step(shard, accum):
        scores = scores_for(key_all, shard)
        probability = jnp.exp(scores - log_total[..., None]).astype(jnp.bfloat16)
        return accum + jnp.einsum(
            "kgqs,skd->qkgd",
            probability,
            value_block(value_all, shard),
            preferred_element_type=jnp.float32,
        )

    attended_f = lax.fori_loop(
        0,
        seq_index + 1,
        out_step,
        jnp.zeros((row_count, KV_HEADS, group_size, HEAD_DIM), jnp.float32),
    )
    attended = (attended_f * out_multiplier).reshape(row_count, q_width).astype(jnp.bfloat16)
    gate_z = projected[:, offset_cols : offset_cols + inner_width]
    xbc_raw = projected[:, offset_cols + inner_width : offset_cols + inner_width + conv_width]
    dt_raw = projected[:, offset_cols + inner_width + conv_width :]
    rim_rows = from_behind(xbc_raw[row_count - (CONV - 1) :], "seq", 1)
    padded = jnp.concatenate([rim_rows, xbc_raw], axis=0)
    (inputs, log_decay, b_matrix, c_matrix, x_heads), pull_prep = jax.vjp(
        prepare, padded, conv_taps, head_params, dt_raw
    )
    (decay_all, end_state), pull_state = jax.vjp(local_state, inputs, log_decay, b_matrix)
    decay_identity = jnp.ones_like(decay_all)
    state_identity = jnp.zeros_like(end_state)
    before_decay, start_state = entering(
        (decay_all, end_state), "seq", chain_step, (decay_identity, state_identity)
    )
    mamba_f, pull_out = jax.vjp(
        mamba_output,
        inputs,
        log_decay,
        b_matrix,
        c_matrix,
        x_heads,
        gate_z,
        head_params,
        gain_mamba,
        start_state,
    )
    joined = jnp.concatenate([attended, mamba_f.astype(jnp.bfloat16)], axis=1)
    hidden = tokens_f + jnp.dot(joined, full_mixout, preferred_element_type=jnp.float32)
    normed2_f, pull_second = jax.vjp(rms_scale, hidden, gain_second)
    normed2 = normed2_f.astype(jnp.bfloat16)
    gate_up = jnp.dot(normed2, full_gateup, preferred_element_type=jnp.float32)
    swiglu_out, pull_swiglu = jax.vjp(swiglu, gate_up)
    activated = swiglu_out.astype(jnp.bfloat16)
    out_block = (hidden + jnp.dot(activated, full_down, preferred_element_type=jnp.float32)).astype(
        jnp.bfloat16
    )
    back_project, back_mixout, back_gateup, back_down = (
        lax.all_gather(w_project.astype(jnp.bfloat16), ("batch", "seq"), axis=0, tiled=True),
        lax.all_gather(w_mixout.astype(jnp.bfloat16), ("batch", "seq"), axis=0, tiled=True),
        lax.all_gather(w_gateup.astype(jnp.bfloat16), ("batch", "seq"), axis=0, tiled=True),
        lax.all_gather(w_down.astype(jnp.bfloat16), ("batch", "seq"), axis=0, tiled=True),
    )
    grad_out = cotangent.astype(jnp.float32)
    grad_down = jnp.einsum("tf,td->fd", activated, cotangent, preferred_element_type=jnp.float32)
    grad_act = jnp.einsum("td,fd->tf", cotangent, back_down, preferred_element_type=jnp.float32)
    (grad_gu_f,) = pull_swiglu(grad_act)
    grad_gu = grad_gu_f.astype(jnp.bfloat16)
    grad_gateup = jnp.einsum("tc,tf->cf", normed2, grad_gu, preferred_element_type=jnp.float32)
    grad_normed2 = jnp.einsum("tf,cf->tc", grad_gu, back_gateup, preferred_element_type=jnp.float32)
    grad_hidden_n, grad_gain_second = pull_second(grad_normed2)
    grad_hidden = grad_out + grad_hidden_n
    grad_branch = grad_hidden.astype(jnp.bfloat16)
    grad_mixout = jnp.einsum("tr,td->rd", joined, grad_branch, preferred_element_type=jnp.float32)
    grad_joined = jnp.einsum(
        "td,rd->tr", grad_branch, back_mixout, preferred_element_type=jnp.float32
    )
    grad_att = (
        grad_joined[:, :q_width]
        .astype(jnp.bfloat16)
        .reshape(row_count, KV_HEADS, group_size, HEAD_DIM)
    )
    grad_mamba = grad_joined[:, q_width:]
    key_back, value_back = (key_all, value_all)
    delta_rows = out_multiplier * jnp.transpose(
        jnp.sum(grad_att.astype(jnp.float32) * attended_f, axis=-1), (1, 2, 0)
    )

    def back_step(shard, carry):
        grad_query, grad_kv = carry
        scores = scores_for(key_back, shard)
        probability = jnp.exp(scores - log_total[..., None])
        value_rows = value_block(value_back, shard)
        key_rows = value_block(key_back, shard)
        grad_probs = out_multiplier * jnp.einsum(
            "qkgd,skd->kgqs", grad_att, value_rows, preferred_element_type=jnp.float32
        )
        grad_scores = (probability * (grad_probs - delta_rows[..., None])).astype(jnp.bfloat16)
        grad_query = grad_query + scale_factor * jnp.einsum(
            "kgqs,skd->qkgd", grad_scores, key_rows, preferred_element_type=jnp.float32
        )
        grad_keys = scale_factor * jnp.einsum(
            "kgqs,qkgd->skd", grad_scores, queries, preferred_element_type=jnp.float32
        )
        grad_values = out_multiplier * jnp.einsum(
            "kgqs,qkgd->skd",
            probability.astype(jnp.bfloat16),
            grad_att,
            preferred_element_type=jnp.float32,
        )
        block_rows = jnp.concatenate(
            [grad_keys.reshape(row_count, kv_width), grad_values.reshape(row_count, kv_width)],
            axis=1,
        )
        grad_kv = lax.dynamic_update_slice_in_dim(grad_kv, block_rows, shard * row_count, 0)
        return (grad_query, grad_kv)

    length_rows = key_back.shape[0]
    grad_query, grad_kv = lax.fori_loop(
        0,
        seq_index + 1,
        back_step,
        (
            jnp.zeros((row_count, KV_HEADS, group_size, HEAD_DIM), jnp.float32),
            jnp.zeros((length_rows, 2 * kv_width), jnp.float32),
        ),
    )
    grad_kv_own = lax.psum_scatter(
        grad_kv.astype(jnp.bfloat16), "seq", scatter_dimension=0, tiled=True
    ).astype(jnp.float32)
    grad_query_pre, grad_key_pre = pull_rope(
        (
            grad_query.reshape(row_count, HEADS, HEAD_DIM),
            grad_kv_own[:, :kv_width].reshape(row_count, KV_HEADS, HEAD_DIM),
        )
    )
    g_inputs, g_logd, g_bmat, g_cmat, g_xheads, g_gate_z, g_head_out, g_gain_mamba, g_start = (
        pull_out(grad_mamba)
    )
    later_decay, carry_grad = entering_2(
        (decay_all, g_start), "seq", chain_step, (decay_identity, state_identity)
    )
    g_decay = jnp.sum(carry_grad * start_state, axis=(1, 2))
    g_inputs_end, g_logd_end, g_bmat_end = pull_state((g_decay, carry_grad))
    g_padded, g_conv, g_head_prep, g_dtraw = pull_prep(
        (g_inputs + g_inputs_end, g_logd + g_logd_end, g_bmat + g_bmat_end, g_cmat, g_xheads)
    )
    back_rim = from_behind(g_padded[: CONV - 1], "seq", -1)
    g_xbc = g_padded[CONV - 1 :]
    g_xbc = jnp.concatenate(
        [g_xbc[: row_count - (CONV - 1)], g_xbc[row_count - (CONV - 1) :] + back_rim], axis=0
    )
    grad_projected = jnp.concatenate(
        [grad_query_pre, grad_key_pre, grad_kv_own[:, kv_width:], g_gate_z, g_xbc, g_dtraw], axis=1
    ).astype(jnp.bfloat16)
    grad_project = jnp.einsum(
        "tc,tk->ck", normed, grad_projected, preferred_element_type=jnp.float32
    )
    grad_normed = jnp.einsum(
        "tk,ck->tc", grad_projected, back_project, preferred_element_type=jnp.float32
    )
    grad_tokens_n, grad_gain_first = pull_first(grad_normed)
    grad_tokens = grad_hidden + grad_tokens_n
    grad_gains = jnp.concatenate([grad_gain_first, grad_gain_second, g_gain_mamba], axis=0)
    own_project, own_mixout, own_gateup, own_down, own_gains, own_conv = (
        lax.psum_scatter(grad_project, ("batch", "seq"), scatter_dimension=0, tiled=True),
        lax.psum_scatter(grad_mixout, ("batch", "seq"), scatter_dimension=0, tiled=True),
        lax.psum_scatter(grad_gateup, ("batch", "seq"), scatter_dimension=0, tiled=True),
        lax.psum_scatter(grad_down, ("batch", "seq"), scatter_dimension=0, tiled=True),
        lax.psum_scatter(grad_gains, ("batch", "seq"), scatter_dimension=0, tiled=True),
        lax.psum_scatter(g_conv, ("batch", "seq"), scatter_dimension=1, tiled=True),
    )
    grad_head = lax.psum(g_head_out + g_head_prep, ("batch", "seq"))
    r_project = adamw_update(
        w_project, own_project, mom_project, sec_project, rate_matrix, weight_decay
    )
    r_mixout = adamw_update(w_mixout, own_mixout, mom_mixout, sec_mixout, rate_matrix, weight_decay)
    r_gateup = adamw_update(w_gateup, own_gateup, mom_gateup, sec_gateup, rate_matrix, weight_decay)
    r_down = adamw_update(w_down, own_down, mom_down, sec_down, rate_matrix, weight_decay)
    r_gains = adamw_update(gains, own_gains, mom_gains, sec_gains, rate_vector, 0.0)
    r_conv = adamw_update(conv_params, own_conv, mom_conv, sec_conv, rate_vector, 0.0)
    r_head = adamw_update(head_params, grad_head, mom_head, sec_head, rate_vector, 0.0)
    return (
        out_block,
        grad_tokens,
        r_project[0],
        r_project[1],
        r_project[2],
        r_mixout[0],
        r_mixout[1],
        r_mixout[2],
        r_gateup[0],
        r_gateup[1],
        r_gateup[2],
        r_down[0],
        r_down[1],
        r_down[2],
        r_gains[0],
        r_gains[1],
        r_gains[2],
        r_conv[0],
        r_conv[1],
        r_conv[2],
        r_head[0],
        r_head[1],
        r_head[2],
    )


def solution(mesh):
    return jax.shard_map(
        local,
        mesh=mesh,
        in_specs=(
            P(("batch", "seq"), None),
            P(("batch", "seq"), None),
            P(("batch", "seq"), None),
            P(("batch", "seq"), None),
            P(("batch", "seq"), None),
            P(("batch", "seq"), None),
            P(("batch", "seq")),
            P(None, ("batch", "seq")),
            P(),
            P(("batch", "seq"), None),
            P(("batch", "seq"), None),
            P(("batch", "seq"), None),
            P(("batch", "seq"), None),
            P(("batch", "seq"), None),
            P(("batch", "seq"), None),
            P(("batch", "seq"), None),
            P(("batch", "seq"), None),
            P(("batch", "seq")),
            P(("batch", "seq")),
            P(None, ("batch", "seq")),
            P(None, ("batch", "seq")),
            P(),
            P(),
        ),
        out_specs=(
            P(("batch", "seq"), None),
            P(("batch", "seq"), None),
            P(("batch", "seq"), None),
            P(("batch", "seq"), None),
            P(("batch", "seq"), None),
            P(("batch", "seq"), None),
            P(("batch", "seq"), None),
            P(("batch", "seq"), None),
            P(("batch", "seq"), None),
            P(("batch", "seq"), None),
            P(("batch", "seq"), None),
            P(("batch", "seq"), None),
            P(("batch", "seq"), None),
            P(("batch", "seq"), None),
            P(("batch", "seq")),
            P(("batch", "seq")),
            P(("batch", "seq")),
            P(None, ("batch", "seq")),
            P(None, ("batch", "seq")),
            P(None, ("batch", "seq")),
            P(),
            P(),
            P(),
        ),
        check_vma=False,
    )
```

profile of v0, /device:TPU:0, one launch (start us, length us, event | category | flops | bytes accessed | tf_op | source)
XLA Modules:
  0.0 1162.7 jit_solution(9367915286352700509)
XLA Ops:
  10.5 43.9 %all-gather.2 = bf16[32,56,5]{1,2,0:T(8,128)(2,1)S(1)} all-gather(bf16[1,56,5]{1,2,0:T(8,128)(2,1)S(1)} %convert_bitcast_fusion), channel_id=1, replica_groups=mesh['batch'=8,'seq'=4] {'batch','seq'}, dimensions={0}, use_global_device_ids=true | all-gather | bytes 18480 | tf_op jit(solution)/shard_map/all_gather | solution.py:212
  54.8 38.8 %all-reduce.23 = bf16[3584]{0:T(1024)(128)(2,1)S(1)} all-reduce(bf16[3584]{0:T(1024)(128)(2,1)S(1)} %dynamic-update-slice), channel_id=1, replica_groups=mesh['batch'=8,'seq'=4] {'batch','seq'}, use_global_device_ids=true, to_apply=%add.23 | all-reduce | flops 3584 | bytes 14336
  94.1 7.2 fusion.124
  110.1 5.9 fusion.56
  117.6 3.0 copy.241
  120.6 3.6 fusion.80
  128.0 2.7 slice.211
  130.9 10.1 all_gather.49
  141.7 2.9 while.66
  144.6 14.7 %all_gather.48 = bf16[1024,128]{0,1:T(8,128)(2,1)} all-gather(bf16[256,128]{0,1:T(8,128)(2,1)S(1)} %slice.330), channel_id=1, replica_groups=mesh['batch'=8,'seq'=4] {'seq'}, dimensions={0}, use_global_device_ids=true | all-gather | bytes 327680 | tf_op jit(solution)/shard_map/all_gather | solution.py:241
  159.4 2.8 while.67
  163.3 12.4 %all-gather.3 = bf16[4,1,24]{2,1,0:T(2,128)(2,1)S(1)} all-gather(bf16[1,1,24]{2,1,0:T(2,128)(2,1)S(1)} %bitcast.405), channel_id=1, replica_groups=mesh['batch'=8,'seq'=4] {'seq'}, dimensions={0}, use_global_device_ids=true | all-gather | bytes 240 | tf_op jit(solution)/shard_map/all_gather | solution.py:38
  175.7 3.0 copy.279
  180.8 7.0 fusion.60
  193.1 18.2 %all-gather.13.cloned.1.call-done = bf16[2048,1024]{1,0:T(8,128)(2,1)} async-done(((bf16[64,1024]{1,0:T(8,128)(2,1)}), bf16[2048,1024]{1,0:T(8,128)(2,1)}) %all-gather.13.cloned.1.call-update) | async-done | bytes 4194320 | tf_op jit(solution)/shard_map/all_gather | solution.py:208
  211.3 3.9 multiply_reduce_fusion.13
  215.3 75.3 %all-gather.15.cloned.1.call-done = bf16[1024,4096]{1,0:T(8,128)(2,1)} async-done(((bf16[32,4096]{1,0:T(8,128)(2,1)}), bf16[1024,4096]{1,0:T(8,128)(2,1)}) %all-gather.15.cloned.1.call-update) | async-done | bytes 8388624 | tf_op jit(solution)/shard_map/all_gather | solution.py:209
  290.6 7.7 fusion.169
  298.3 56.2 %all-gather.17.cloned.1.call-done = bf16[2048,1024]{1,0:T(8,128)(2,1)} async-done(((bf16[64,1024]{1,0:T(8,128)(2,1)}), bf16[2048,1024]{1,0:T(8,128)(2,1)}) %all-gather.17.cloned.1.call-update) | async-done | bytes 4194320 | tf_op jit(solution)/shard_map/all_gather | solution.py:210
  354.6 17.9 %fusion.121 = (f32[256,2048]{1,0:T(8,128)S(1)}, f32[256,2048]{1,0:T(8,128)S(1)}, bf16[256,2048]{1,0:T(8,128)(2,1)}) fusion(f32[256,4096]{1,0:T(8,128)} %fusion.169, bf16[256,1024]{1,0:T(8,128)(2,1)} %param.34, bf16[2048,1024]{1,0:T(8,128)(2,1)} %all-gather.17.cloned.1.call-done), kind=kOutput, calls=%fused_computation.213 | convolution fusion | flops 1081081856 | bytes 14155776 | tf_op jit(solution)/shard_map/td,fd->tf/dot_general | solution.py:335
  372.5 4.1 multiply_reduce_fusion.11
  384.5 11.4 while.68
  398.5 4.5 multiply_reduce_fusion.4
  403.0 3.1 copy.251
  406.1 3.6 fusion.83
  409.8 5.8 fusion.110
  416.7 5.8 fusion.183
  427.1 4.0 fusion.91
  431.2 11.1 fusion.38
  444.2 6.1 reduce-scatter.7.cloned.1.call-done
  456.7 4.4 fusion.109
  461.1 11.2 all-gather.21.cloned.1.call-done
  472.3 4.9 while.69
  479.8 9.0 multiply_reduce_fusion.6
  489.5 3.2 reduce-window.24
  493.6 2.7 reduce-window.26
  497.4 3.1 copy.252
  500.5 2.6 fusion.88
  504.7 3.1 multiply_reduce_fusion.2
  514.0 8.6 fusion.122
  523.8 10.5 fusion.113
  535.6 4.4 fusion.79
  540.3 6.3 fusion.95
  546.6 58.0 %all-reduce.26 = (f32[3584]{0:T(1024)S(1)}, f32[5,1792]{1,0:T(8,128)S(1)}, f32[3,24]{1,0:T(4,128)S(1)}) all-reduce(f32[3584]{0:T(1024)S(1)} %pad_maximum_fusion.7, f32[5,1792]{1,0:T(8,128)S(1)} %pad_add_fusion.1, f32[3,24]{1,0:T(4,128)S(1)} %add_add_fusion.5), channel_id=9, replica_groups=mesh['batch'=8,'seq'=4] {'batch','seq'}, use_global_device_ids=true, to_apply=%region_41.42.clone | all-reduce | flops 12616 | bytes 100928
  608.0 15.7 %reduce-scatter.11.cloned.1.call-done = f32[64,1024]{1,0:T(8,128)} async-done(((f32[2048,1024]{1,0:T(8,128)}), f32[64,1024]{1,0:T(8,128)}) %reduce-scatter.11.cloned.1.call-update) | async-done | bytes 262160 | tf_op jit(solution)/shard_map/reduce_scatter | solution.py:436
  625.7 145.1 %reduce-scatter.15.cloned.1.call-done = f32[64,1024]{1,0:T(8,128)} async-done(((f32[2048,1024]{1,0:T(8,128)}), f32[64,1024]{1,0:T(8,128)}) %reduce-scatter.15.cloned.1.call-update) | async-done | bytes 262160 | tf_op jit(solution)/shard_map/reduce_scatter | solution.py:438
  772.9 196.5 %reduce-scatter.9.cloned.1.call-done = f32[32,4120]{1,0:T(8,128)} async-done(((f32[1024,4120]{1,0:T(8,128)}), f32[32,4120]{1,0:T(8,128)}) %reduce-scatter.9.cloned.1.call-update) | async-done | bytes 527376 | tf_op jit(solution)/shard_map/reduce_scatter | solution.py:435
  971.8 181.7 %reduce-scatter.13.cloned.1.call-done = f32[32,4096]{1,0:T(8,128)} async-done(((f32[1024,4096]{1,0:T(8,128)}), f32[32,4096]{1,0:T(8,128)}) %reduce-scatter.13.cloned.1.call-update) | async-done | bytes 524304 | tf_op jit(solution)/shard_map/reduce_scatter | solution.py:437
  (427 shorter events, 100.5 us)
Async XLA Ops:
  7.2 86.5 %copy-start.15 = (bf16[256,1024]{1,0:T(8,128)(2,1)S(1)}, bf16[256,1024]{1,0:T(8,128)(2,1)}, u32[]{:S(2)}) copy-start(bf16[256,1024]{1,0:T(8,128)(2,1)} %param.33) | copy-start | bytes 1572868
  7.2 86.8 %copy-start.99 = (f32[3,24]{1,0:T(4,128)S(1)}, f32[3,24]{1,0:T(4,128)}, u32[]{:S(2)}) copy-start(f32[3,24]{1,0:T(4,128)} %param.41) | copy-start | bytes 868
  7.2 86.8 %all-gather.11.cloned.1.call-start = ((), (), s32[]{:S(2)}) async-start(), calls=%async_computation.5 | async-start | bytes 8921088 | tf_op jit(solution)/shard_map/all_gather | solution.py:207
  9.1 170.1 %all-gather.19.cloned.1.call-start = ((), (), s32[]{:S(2)}) async-start(), calls=%async_computation.14 | async-start | bytes 1966080 | tf_op jit(solution)/shard_map/all_gather | solution.py:38
  93.7 16.4 %copy-start.68 = (f32[1792]{0:T(1024)}, f32[1792]{0:T(1024)S(1)}, u32[]{:S(2)}) copy-start(f32[1792]{0:T(1024)S(1)} %get-tuple-element.473) | copy-start | bytes 21508
  93.7 16.4 %copy-start.70 = (f32[1792]{0:T(1024)}, f32[1792]{0:T(1024)S(1)}, u32[]{:S(2)}) copy-start(f32[1792]{0:T(1024)S(1)} %get-tuple-element.474) | copy-start | bytes 21508
  94.0 86.8 %copy-start.112 = (f32[24]{0:T(128)}, f32[24]{0:T(128)S(1)}, u32[]{:S(2)}) copy-start(f32[24]{0:T(128)S(1)} %get-tuple-element.618) | copy-start | bytes 292
  104.8 76.0 %copy-start.63 = (f32[256,24]{0,1:T(8,128)}, f32[256,24]{0,1:T(8,128)S(1)}, u32[]{:S(2)}) copy-start(f32[256,24]{0,1:T(8,128)S(1)} %bitcast_bitcast_fusion) | copy-start | bytes 73732
  105.3 4.7 collective-permute-start
  106.8 74.0 %copy-start.59 = (f32[256,24]{0,1:T(8,128)}, f32[256,24]{0,1:T(8,128)S(1)}, u32[]{:S(2)}) copy-start(f32[256,24]{0,1:T(8,128)S(1)} %get-tuple-element.614) | copy-start | bytes 73732
  110.0 70.8 %copy-start.56 = (f32[256,24]{0,1:T(8,128)}, f32[256,24]{0,1:T(8,128)S(1)}, u32[]{:S(2)}) copy-start(f32[256,24]{0,1:T(8,128)S(1)} %copy.237) | copy-start | bytes 73732
  116.0 63.3 %copy-start.2 = (f32[256,1792]{1,0:T(8,128)}, f32[256,1792]{1,0:T(8,128)S(1)}, u32[]{:S(2)}) copy-start(f32[256,1792]{1,0:T(8,128)S(1)} %get-tuple-element.580) | copy-start | bytes 5505028
  124.3 87.0 %all-gather.13.cloned.1.call-start = ((), (), s32[]{:S(2)}) async-start(), calls=%async_computation.6 | async-start | bytes 4325376 | tf_op jit(solution)/shard_map/all_gather | solution.py:208
  125.1 165.5 %all-gather.15.cloned.1.call-start = ((), (), s32[]{:S(2)}) async-start(), calls=%async_computation.7 | async-start | bytes 8650752 | tf_op jit(solution)/shard_map/all_gather | solution.py:209
  125.9 228.7 %all-gather.17.cloned.1.call-start = ((), (), s32[]{:S(2)}) async-start(), calls=%async_computation.8 | async-start | bytes 4325376 | tf_op jit(solution)/shard_map/all_gather | solution.py:210
  126.6 323.7 %reduce-scatter.7.cloned.1.call-start = ((), (), s32[]{:S(2)}) async-start(), calls=%async_computation.9 | async-start | bytes 655360 | tf_op jit(solution)/shard_map/reduce_scatter | solution.py:397
  126.7 54.1 %copy-start.76 = (pred[256,256]{1,0:T(8,128)(4,1)}, pred[256,256]{1,0:T(8,128)(4,1)S(1)}, u32[]{:S(2)}) copy-start(pred[256,256]{1,0:T(8,128)(4,1)S(1)} %iota_compare_fusion) | copy-start | bytes 196612
  126.8 65.2 %copy-start.61 = (f32[1536]{0:T(1024)}, f32[1536]{0:T(1024)S(1)}, u32[]{:S(2)}) copy-start(f32[1536]{0:T(1024)S(1)} %slice.212) | copy-start | bytes 18436
  162.2 16.5 %copy-start.17 = (f32[256,2,4,64]{0,3,2,1:T(8,128)}, f32[256,2,4,64]{0,3,2,1:T(8,128)S(1)}, u32[]{:S(2)}) copy-start(f32[256,2,4,64]{0,3,2,1:T(8,128)S(1)} %get-tuple-element.342) | copy-start | bytes 1572868
  215.2 161.4 %copy-start.11 = (f32[256,1024]{1,0:T(8,128)}, f32[256,1024]{1,0:T(8,128)S(1)}, u32[]{:S(2)}) copy-start(f32[256,1024]{1,0:T(8,128)S(1)} %get-tuple-element.624) | copy-start | bytes 3145732
  215.3 161.4 %copy-start.79 = (f32[256]{0:T(256)}, f32[256]{0:T(256)S(1)}, u32[]{:S(2)}) copy-start(f32[256]{0:T(256)S(1)} %fusion.159) | copy-start | bytes 3076
  354.5 17.9 %copy-start.10 = (bf16[1024,4096]{1,0:T(8,128)(2,1)S(1)}, bf16[1024,4096]{1,0:T(8,128)(2,1)}, u32[]{:S(2)}) copy-start(bf16[1024,4096]{1,0:T(8,128)(2,1)} %all-gather.15.cloned.1.call-done) | copy-start | bytes 25165828
  395.9 76.4 %all-gather.21.cloned.1.call-start = ((), (), s32[]{:S(2)}) async-start(), calls=%async_computation.15 | async-start | bytes 1966080 | tf_op jit(solution)/shard_map/all_gather | solution.py:58
  409.8 213.9 %reduce-scatter.11.cloned.1.call-start = ((), (), s32[]{:S(2)}) async-start(), calls=%async_computation.11 | async-start | bytes 8650752 | tf_op jit(solution)/shard_map/reduce_scatter | solution.py:436
  415.6 355.1 %reduce-scatter.15.cloned.1.call-start = ((), (), s32[]{:S(2)}) async-start(), calls=%async_computation.13 | async-start | bytes 8650752 | tf_op jit(solution)/shard_map/reduce_scatter | solution.py:438
  422.5 546.8 %reduce-scatter.9.cloned.1.call-start = ((), (), s32[]{:S(2)}) async-start(), calls=%async_computation.10 | async-start | bytes 17842176 | tf_op jit(solution)/shard_map/reduce_scatter | solution.py:435
  508.5 3.2 collective-permute-start.1
  522.6 630.9 %reduce-scatter.13.cloned.1.call-start = ((), (), s32[]{:S(2)}) async-start(), calls=%async_computation.12 | async-start | bytes 17301504 | tf_op jit(solution)/shard_map/reduce_scatter | solution.py:437
  540.2 64.5 %copy-start.94 = (f32[256]{0:T(256)S(1)}, f32[256]{0:T(256)}, u32[]{:S(2)}) copy-start(f32[256]{0:T(256)} %copy-done.93) | copy-start | bytes 3076
  540.2 64.5 %copy-start.114 = (f32[112]{0:T(128)S(1)}, f32[112]{0:T(128)}, u32[]{:S(2)}) copy-start(f32[112]{0:T(128)} %param.39) | copy-start | bytes 1348
  540.2 64.5 %copy-start.115 = (f32[112]{0:T(128)S(1)}, f32[112]{0:T(128)}, u32[]{:S(2)}) copy-start(f32[112]{0:T(128)} %param.51) | copy-start | bytes 1348
  540.2 64.5 %copy-start.116 = (f32[112]{0:T(128)S(1)}, f32[112]{0:T(128)}, u32[]{:S(2)}) copy-start(f32[112]{0:T(128)} %param.50) | copy-start | bytes 1348
  540.2 65.1 %copy-start.108 = (f32[3,24]{1,0:T(4,128)S(1)}, f32[3,24]{1,0:T(4,128)}, u32[]{:S(2)}) copy-start(f32[3,24]{1,0:T(4,128)} %param.55) | copy-start | bytes 868
  540.2 65.1 %copy-start.109 = (f32[3,24]{1,0:T(4,128)S(1)}, f32[3,24]{1,0:T(4,128)}, u32[]{:S(2)}) copy-start(f32[3,24]{1,0:T(4,128)} %param.54) | copy-start | bytes 868
  540.2 65.7 %copy-start.91 = (f32[5,56]{1,0:T(8,128)S(1)}, f32[5,56]{1,0:T(8,128)}, u32[]{:S(2)}) copy-start(f32[5,56]{1,0:T(8,128)} %param.40) | copy-start | bytes 3364
  540.2 65.7 %copy-start.105 = (f32[5,56]{1,0:T(8,128)S(1)}, f32[5,56]{1,0:T(8,128)}, u32[]{:S(2)}) copy-start(f32[5,56]{1,0:T(8,128)} %param.53) | copy-start | bytes 3364
  540.3 65.7 %copy-start.106 = (f32[5,56]{1,0:T(8,128)S(1)}, f32[5,56]{1,0:T(8,128)}, u32[]{:S(2)}) copy-start(f32[5,56]{1,0:T(8,128)} %param.52) | copy-start | bytes 3364
  540.3 66.4 %copy-start.5 = (f32[256,1024]{1,0:T(8,128)S(1)}, f32[256,1024]{1,0:T(8,128)}, u32[]{:S(2)}) copy-start(f32[256,1024]{1,0:T(8,128)} %copy-done.3) | copy-start | bytes 3145732
  606.7 17.0 %copy-start.35 = (f32[64,1024]{1,0:T(8,128)S(1)}, f32[64,1024]{1,0:T(8,128)}, u32[]{:S(2)}) copy-start(f32[64,1024]{1,0:T(8,128)} %param.36) | copy-start | bytes 786436
  606.7 17.0 %copy-start.51 = (f32[64,1024]{1,0:T(8,128)S(1)}, f32[64,1024]{1,0:T(8,128)}, u32[]{:S(2)}) copy-start(f32[64,1024]{1,0:T(8,128)} %param.45) | copy-start | bytes 786436
  606.7 17.0 %copy-start.52 = (f32[64,1024]{1,0:T(8,128)S(1)}, f32[64,1024]{1,0:T(8,128)}, u32[]{:S(2)}) copy-start(f32[64,1024]{1,0:T(8,128)} %param.44) | copy-start | bytes 786436
  608.0 162.8 %copy-start.37 = (f32[64,1024]{1,0:T(8,128)S(1)}, f32[64,1024]{1,0:T(8,128)}, u32[]{:S(2)}) copy-start(f32[64,1024]{1,0:T(8,128)} %param.38) | copy-start | bytes 786436
  608.0 361.4 %copy-start.23 = (f32[32,4120]{1,0:T(8,128)S(1)}, f32[32,4120]{1,0:T(8,128)}, u32[]{:S(2)}) copy-start(f32[32,4120]{1,0:T(8,128)} %param.35) | copy-start | bytes 1582084
  608.0 361.4 %copy-start.46 = (f32[32,4120]{1,0:T(8,128)S(1)}, f32[32,4120]{1,0:T(8,128)}, u32[]{:S(2)}) copy-start(f32[32,4120]{1,0:T(8,128)} %param.43) | copy-start | bytes 1582084
  608.0 361.4 %copy-start.47 = (f32[32,4120]{1,0:T(8,128)S(1)}, f32[32,4120]{1,0:T(8,128)}, u32[]{:S(2)}) copy-start(f32[32,4120]{1,0:T(8,128)} %param.42) | copy-start | bytes 1582084
  772.9 380.6 %copy-start.25 = (f32[32,4096]{1,0:T(8,128)S(1)}, f32[32,4096]{1,0:T(8,128)}, u32[]{:S(2)}) copy-start(f32[32,4096]{1,0:T(8,128)} %param.37) | copy-start | bytes 1572868
  772.9 380.6 %copy-start.49 = (f32[32,4096]{1,0:T(8,128)S(1)}, f32[32,4096]{1,0:T(8,128)}, u32[]{:S(2)}) copy-start(f32[32,4096]{1,0:T(8,128)} %param.47) | copy-start | bytes 1572868
  772.9 380.6 %copy-start.50 = (f32[32,4096]{1,0:T(8,128)S(1)}, f32[32,4096]{1,0:T(8,128)}, u32[]{:S(2)}) copy-start(f32[32,4096]{1,0:T(8,128)} %param.46) | copy-start | bytes 1572868
  (85 other events, 366.2 us)
Sparse Core Ops, SparseCore 0:
  11.5 81.5 all-gather.10
  124.4 22.0 all-gather.18
  150.0 61.2 all-gather.12
  214.6 75.9 all-gather.14
  293.9 60.6 all-gather.16
  396.0 54.2 reduce-scatter.6
  452.6 19.6 all-gather.20
  474.7 148.9 reduce-scatter.10
  626.1 144.6 reduce-scatter.14
  778.2 191.1 reduce-scatter.8
  971.7 181.7 reduce-scatter.12
where the time goes:
time: 1170 us; the launch traced here: 1160 us
  waiting for transfers between devices  707 us (60%)
  blocking collectives  178 us (15%)
  matrix products  144 us (12%)
  other arithmetic  64.9 us (6%)
  local copies, waits for them, and re-layouts  49.6 us (4%)
  between operations  15.8 us (1%)
    reduce_scatter x1, waiting for transfers between devices, local(): lax.psum_scatter(grad_project, ('batch', 'seq'), scatter_dimension=0, til...  196 us
    reduce_scatter x1, waiting for transfers between devices, local(): lax.psum_scatter(grad_gateup, ('batch', 'seq'), scatter_dimension=0, tile...  182 us
    reduce_scatter x1, waiting for transfers between devices, local(): lax.psum_scatter(grad_down, ('batch', 'seq'), scatter_dimension=0, tiled=...  145 us
    unnamed x2, blocking collectives  96.9 us
    all_gather x1, waiting for transfers between devices, local(): lax.all_gather(w_gateup.astype(jnp.bfloat16), ('batch', 'seq'), axis=0, t...  75.3 us
    all_gather x1, waiting for transfers between devices, local(): lax.all_gather(w_down.astype(jnp.bfloat16), ('batch', 'seq'), axis=0, til...  56.2 us
    all_gather x1, blocking collectives, local(): lax.all_gather(conv_params.astype(jnp.bfloat16), ('batch', 'seq'), axis=1...  43.9 us
    dot_general x3, matrix products, mamba_output(): within = jnp.einsum('tsh,shp->thp', mixing, inputs, precision=highest)  27.1 us
  transfers between devices with their start and end apart: 13, of which 10 were waited for; matrix products, arithmetic and copies ran while one was open for 15% of the time, Pallas kernels for 0%

commit v1 on v0

--- a/solution.py
+++ b/solution.py
@@ -167,6 +167,33 @@
         corrected_one / (jnp.sqrt(corrected_two) + adam_eps) + decay * weight
     )
     return (moment_one, moment_two, new_weight)
+
+
+def pack_project(weights, gains, taps):
+    rows = weights.shape[0]
+    vectors = jnp.concatenate([gains, taps.reshape(-1)])
+    width = -(-vectors.shape[0] // rows)
+    vectors = jnp.pad(vectors, (0, width * rows - vectors.shape[0])).reshape(rows, width)
+    return jnp.concatenate([weights, vectors], axis=1).astype(jnp.bfloat16)
+
+
+def pack_late(weights, gains, taps, devices):
+    rows = weights.shape[0] // devices
+    split_taps = jnp.transpose(taps.reshape(CONV + 1, devices, -1), (1, 0, 2))
+    vectors = jnp.concatenate([gains.reshape(devices, -1), split_taps.reshape(devices, -1)], axis=1)
+    width = -(-vectors.shape[1] // rows)
+    vectors = jnp.pad(vectors, ((0, 0), (0, width * rows - vectors.shape[1])))
+    return jnp.concatenate([weights, vectors.reshape(devices * rows, width)], axis=1).astype(
+        jnp.bfloat16
+    )
+
+
+def unpack_vectors(packed, start, devices, gains, taps):
+    vectors = packed[:, start:].reshape(devices, -1)
+    count = gains.shape[0]
+    own_gains = vectors[:, :count].reshape(-1)
+    own_taps = vectors[:, count : count + taps.size].reshape(devices, CONV + 1, taps.shape[1])
+    return own_gains, jnp.transpose(own_taps, (1, 0, 2)).reshape(CONV + 1, -1)
 
 
 def local(
@@ -203,13 +230,17 @@
     conv_width = inner_width + 2 * STATE
     offset_cols = q_width + 2 * kv_width
     out_multiplier = (row_count * lax.axis_size("seq") / 6.0) ** 0.5
-    full_project, full_mixout, full_gateup, full_down, full_gains, full_conv = (
-        lax.all_gather(w_project.astype(jnp.bfloat16), ("batch", "seq"), axis=0, tiled=True),
+    devices = lax.axis_size("batch") * lax.axis_size("seq")
+    share = w_project.shape[0]
+    full_packed = lax.all_gather(
+        pack_project(w_project, gains, conv_params), ("batch", "seq"), axis=0, tiled=True
+    )
+    full_project = full_packed[:, : w_project.shape[1]]
+    full_gains, full_conv = unpack_vectors(full_packed, w_project.shape[1], devices, gains, conv_params)
+    full_mixout, full_gateup, full_down = (
         lax.all_gather(w_mixout.astype(jnp.bfloat16), ("batch", "seq"), axis=0, tiled=True),
         lax.all_gather(w_gateup.astype(jnp.bfloat16), ("batch", "seq"), axis=0, tiled=True),
         lax.all_gather(w_down.astype(jnp.bfloat16), ("batch", "seq"), axis=0, tiled=True),
-        lax.all_gather(gains.astype(jnp.bfloat16), ("batch", "seq"), axis=0, tiled=True),
-        lax.all_gather(conv_params.astype(jnp.bfloat16), ("batch", "seq"), axis=1, tiled=True),
     )
     gains_f = full_gains.astype(jnp.float32)
     gain_first = gains_f[:D]
@@ -325,10 +356,10 @@
         jnp.bfloat16
     )
     back_project, back_mixout, back_gateup, back_down = (
-        lax.all_gather(w_project.astype(jnp.bfloat16), ("batch", "seq"), axis=0, tiled=True),
-        lax.all_gather(w_mixout.astype(jnp.bfloat16), ("batch", "seq"), axis=0, tiled=True),
-        lax.all_gather(w_gateup.astype(jnp.bfloat16), ("batch", "seq"), axis=0, tiled=True),
-        lax.all_gather(w_down.astype(jnp.bfloat16), ("batch", "seq"), axis=0, tiled=True),
+        full_project,
+        full_mixout,
+        full_gateup,
+        full_down,
     )
     grad_out = cotangent.astype(jnp.float32)
     grad_down = jnp.einsum("tf,td->fd", activated, cotangent, preferred_element_type=jnp.float32)
@@ -341,6 +372,13 @@
     grad_hidden = grad_out + grad_hidden_n
     grad_branch = grad_hidden.astype(jnp.bfloat16)
     grad_mixout = jnp.einsum("tr,td->rd", joined, grad_branch, preferred_element_type=jnp.float32)
+    pair = jnp.stack([grad_mixout, grad_down], axis=0).astype(jnp.bfloat16)
+    pair = jnp.transpose(pair.reshape(2, devices, 2, share, D), (1, 3, 2, 0, 4))
+    early = jnp.concatenate(
+        [grad_gateup.astype(jnp.bfloat16), pair.reshape(devices * share, 4 * D)], axis=1
+    )
+    early, grad_branch = lax.optimization_barrier((early, grad_branch))
+    own_early = lax.psum_scatter(early, ("batch", "seq"), scatter_dimension=0, tiled=True)
     grad_joined = jnp.einsum(
         "td,rd->tr", grad_branch, back_mixout, preferred_element_type=jnp.float32
     )
@@ -431,15 +469,18 @@
     grad_tokens_n, grad_gain_first = pull_first(grad_normed)
     grad_tokens = grad_hidden + grad_tokens_n
     grad_gains = jnp.concatenate([grad_gain_first, grad_gain_second, g_gain_mamba], axis=0)
-    own_project, own_mixout, own_gateup, own_down, own_gains, own_conv = (
-        lax.psum_scatter(grad_project, ("batch", "seq"), scatter_dimension=0, tiled=True),
-        lax.psum_scatter(grad_mixout, ("batch", "seq"), scatter_dimension=0, tiled=True),
-        lax.psum_scatter(grad_gateup, ("batch", "seq"), scatter_dimension=0, tiled=True),
-        lax.psum_scatter(grad_down, ("batch", "seq"), scatter_dimension=0, tiled=True),
-        lax.psum_scatter(grad_gains, ("batch", "seq"), scatter_dimension=0, tiled=True),
-        lax.psum_scatter(g_conv, ("batch", "seq"), scatter_dimension=1, tiled=True),
-    )
+    late = pack_late(grad_project, grad_gains, g_conv, devices)
+    own_late = lax.psum_scatter(late, ("batch", "seq"), scatter_dimension=0, tiled=True).astype(
+        jnp.float32
+    )
+    own_project = own_late[:, : w_project.shape[1]]
+    own_gains, own_conv = unpack_vectors(own_late, w_project.shape[1], 1, gains, conv_params)
     grad_head = lax.psum(g_head_out + g_head_prep, ("batch", "seq"))
+    own_early = own_early.astype(jnp.float32)
+    own_gateup = own_early[:, : 2 * FF]
+    own_pair = own_early[:, 2 * FF :].reshape(share, 2, 2, D)
+    own_pair = jnp.transpose(own_pair, (2, 1, 0, 3)).reshape(2, 2 * share, D)
+    own_mixout, own_down = own_pair[0], own_pair[1]
     r_project = adamw_update(
         w_project, own_project, mom_project, sec_project, rate_matrix, weight_decay
     )

time: 1170 us -> 988 us (0.84)
  waiting for transfers between devices: 707 us -> 524 us
  blocking collectives: 178 us -> 63.8 us
  local copies, waits for them, and re-layouts: 49.6 us -> 125 us
  other arithmetic: 64.9 us -> 114 us
  matrix products: 144 us -> 132 us
    reduce_scatter x4 -> x2, waiting for transfers between devices: 539 us -> 261 us  [the longest x1 178 us: local(): lax.psum_scatter(early, ('batch', 'seq'), scatter_dimension=0, tiled=True)]
    unnamed x2 -> x0, blocking collectives: 96.9 us -> none
    all_gather x1, waiting for transfers between devices: 0.02 us -> 81.1 us  [local(): lax.all_gather(pack_project(w_project, gains, conv_params), ('batch', 'se...]
    all_gather x1 -> x0, blocking collectives: 43.9 us -> none  [local(): lax.all_gather(conv_params.astype(jnp.bfloat16), ('batch', 'seq'), axis=1...]
    psum x0 -> x1, blocking collectives: none -> 41.5 us  [local(): grad_head = lax.psum(g_head_out + g_head_prep, ('batch', 'seq'))]
    another operation x7 -> x10, local copies, waits for them, and re-layouts: 1.07 us -> 37.5 us  [the longest x2 35.5 us: local(): pair = jnp.stack([grad_mixout, grad_down], axis=0).astype(jnp.bfloat16)]
    concatenate x0 -> x5, other arithmetic: none -> 21.9 us  [the longest x1 13.7 us: local(): jnp.concatenate([grad_gateup.astype(jnp.bfloat16), pair.reshape(devices *...]
    transpose x0 -> x1, other arithmetic: none -> 20.3 us  [local(): pair = jnp.transpose(pair.reshape(2, devices, 2, share, D), (1, 3, 2, 0, 4))]
  transfers between devices with their start and end apart: 13 -> 11, of which waited for: 10 -> 8; matrix products, arithmetic and copies ran while one was open for 15% -> 13% of each run, Pallas kernels for 0% -> 0%
where the time goes in v1:
time: 988 us; the launch traced here: 980 us
  waiting for transfers between devices  524 us (53%)
  matrix products  132 us (13%)
  local copies, waits for them, and re-layouts  125 us (13%)
  other arithmetic  114 us (12%)
  blocking collectives  63.8 us (6%)
  between operations  15.7 us (2%)
    reduce_scatter x1, waiting for transfers between devices, local(): lax.psum_scatter(early, ('batch', 'seq'), scatter_dimension=0, tiled=True)  178 us
    reduce_scatter x1, waiting for transfers between devices, local(): lax.psum_scatter(late, ('batch', 'seq'), scatter_dimension=0, tiled=True)  83 us
    all_gather x1, waiting for transfers between devices, local(): lax.all_gather(pack_project(w_project, gains, conv_params), ('batch', 'se...  81.1 us
    all_gather x1, waiting for transfers between devices, local(): lax.all_gather(w_gateup.astype(jnp.bfloat16), ('batch', 'seq'), axis=0, t...  74.5 us
    all_gather x1, waiting for transfers between devices, local(): lax.all_gather(w_down.astype(jnp.bfloat16), ('batch', 'seq'), axis=0, til...  55.8 us
    psum x1, blocking collectives, local(): grad_head = lax.psum(g_head_out + g_head_prep, ('batch', 'seq'))  41.5 us
    another operation x2, local copies, waits for them, and re-layouts, local(): pair = jnp.stack([grad_mixout, grad_down], axis=0).astype(jnp.bfloat16)  35.5 us
    unnamed x232, local copies, waits for them, and re-layouts  29.5 us
  transfers between devices with their start and end apart: 11, of which 8 were waited for; matrix products, arithmetic and copies ran while one was open for 13% of the time, Pallas kernels for 0%

profile of v1, /device:TPU:0, one launch (start us, length us, event | category | flops | bytes accessed | tf_op | source)
XLA Modules:
  0.0 979.8 jit_solution(865103679662893048)
XLA Ops:
  11.6 81.1 %all-gather.10.cloned.1.call-done = bf16[1024,4133]{1,0:T(8,128)(2,1)} async-done(((bf16[32,4133]{1,0:T(8,128)(2,1)}), bf16[1024,4133]{1,0:T(8,128)(2,1)}) %all-gather.10.cloned.1.call-update) | async-done | bytes 8464400 | tf_op jit(solution)/shard_map/all_gather | solution.py:235
  94.3 7.2 fusion.31
  111.6 6.0 fusion.60
  119.2 3.0 copy.314
  122.2 3.6 fusion.84
  131.4 7.9 all_gather.38
  141.3 9.4 all_gather.37
  153.4 5.0 all-gather.2
  158.4 3.1 copy.359
  162.3 3.7 while.67
  172.5 7.0 fusion.64
  184.8 25.8 %all-gather.12.cloned.1.call-done = bf16[2048,1024]{1,0:T(8,128)(2,1)} async-done(((bf16[64,1024]{1,0:T(8,128)(2,1)}), bf16[2048,1024]{1,0:T(8,128)(2,1)}) %all-gather.12.cloned.1.call-update) | async-done | bytes 4194320 | tf_op jit(solution)/shard_map/all_gather | solution.py:241
  210.6 4.8 multiply_reduce_fusion.13
  215.4 74.5 %all-gather.14.cloned.1.call-done = bf16[1024,4096]{1,0:T(8,128)(2,1)} async-done(((bf16[32,4096]{1,0:T(8,128)(2,1)}), bf16[1024,4096]{1,0:T(8,128)(2,1)}) %all-gather.14.cloned.1.call-update) | async-done | bytes 8388624 | tf_op jit(solution)/shard_map/all_gather | solution.py:242
  289.9 8.1 fusion.174
  298.0 55.8 %all-gather.16.cloned.1.call-done = bf16[2048,1024]{1,0:T(8,128)(2,1)} async-done(((bf16[64,1024]{1,0:T(8,128)(2,1)}), bf16[2048,1024]{1,0:T(8,128)(2,1)}) %all-gather.16.cloned.1.call-update) | async-done | bytes 4194320 | tf_op jit(solution)/shard_map/all_gather | solution.py:243
  353.9 17.2 %fusion.122 = (f32[256,2048]{1,0:T(8,128)S(1)}, f32[256,2048]{1,0:T(8,128)}, bf16[256,2048]{1,0:T(8,128)(2,1)S(1)}) fusion(f32[256,4096]{1,0:T(8,128)} %fusion.174, bf16[256,1024]{1,0:T(8,128)(2,1)} %param.34, bf16[2048,1024]{1,0:T(8,128)(2,1)} %all-gather.16.cloned.1.call-done), kind=kOutput, calls=%fused_computation.222 | convolution fusion | flops 1081081856 | bytes 14155776 | tf_op jit(solution)/shard_map/td,fd->tf/dot_general | solution.py:366
  372.4 17.8 %copy.321 = bf16[1,32,2,32,1024]{4,0,2,3,1:T(2,128)(2,1)S(1)} copy(bf16[1,32,2,32,1024]{4,3,2,1,0:T(8,128)(2,1)S(1)} %bitcast.382) | data formatting | bytes 8388608 | tf_op jit(solution)/shard_map/stack | solution.py:375
  390.2 7.5 convolution_convert_fusion.1
  397.7 6.7 multiply_reduce_fusion.11
  407.2 17.8 %copy.320 = bf16[1,32,2,32,1024]{4,0,2,3,1:T(2,128)(2,1)S(1)} copy(bf16[1,32,2,32,1024]{4,3,2,1,0:T(8,128)(2,1)S(1)} %bitcast.400) | data formatting | bytes 8388608 | tf_op jit(solution)/shard_map/stack | solution.py:375
  424.9 20.3 %maximum_bitcast_fusion = bf16[32,32,2,2,1024]{4,3,2,1,0:T(2,128)(2,1)} fusion(bf16[1,32,2,32,1024]{4,0,2,3,1:T(2,128)(2,1)S(1)} %copy.321, bf16[1,32,2,32,1024]{4,0,2,3,1:T(2,128)(2,1)S(1)} %copy.320), kind=kLoop, calls=%fused_computation.58 | loop fusion | flops 16777216 | bytes 16777216 | tf_op jit(solution)/shard_map/transpose | solution.py:376
  445.2 14.4 %reshape.465 = bf16[1024,4096]{1,0:T(8,128)(2,1)} reshape(bf16[32,32,2,2,1024]{4,3,2,1,0:T(2,128)(2,1)} %maximum_bitcast_fusion) | data formatting | bytes 16777216 | tf_op jit(solution)/shard_map/reshape | solution.py:378
  459.7 13.7 %pad_maximum_fusion.1 = bf16[1024,8192]{1,0:T(8,128)(2,1)} fusion(bf16[1024,4096]{1,0:T(8,128)(2,1)} %reshape.465, bf16[1024,4096]{1,0:T(8,128)(2,1)} %convolution_convert_fusion.1), kind=kLoop, calls=%fused_computation.55 | loop fusion | flops 33554432 | bytes 33554432 | tf_op jit(solution)/shard_map/concatenate | solution.py:377
  473.4 3.6 fusion.192
  483.4 8.5 while.68
  492.9 5.0 multiply_reduce_fusion.4
  499.7 3.0 copy.326
  502.8 3.6 fusion.87
  506.4 11.0 %fusion.42 = (f32[256,24]{0,1:T(8,128)}, f32[256,24]{0,1:T(8,128)}, f32[256,256]{1,0:T(8,128)}) fusion(f32[256,24]{0,1:T(8,128)} %copy-done.63, f32[256,256]{1,0:T(8,128)} %fusion.140, pred[256,256]{1,0:T(8,128)(4,1)} %iota_compare_fusion, f32[24,64,256]{2,1,0:T(8,128)} %bitcast.389, f32[256,24,64]{0,2,1:T(8,128)} %bitcast.384, f32[256,24]{0,1:T(8,128)S(1)} %copy-done.57), kind=kOutput, calls=%fused_computation.75 | convolution fusion | flops 1222430720 | bytes 3833856 | tf_op jit(solution)/shard_map/transpose(jvp(tsh,shp->thp))/dot_general | solution.py:143
  522.7 4.1 fusion.95
  528.8 8.9 reduce-scatter.6.cloned.1.call-done
  540.9 4.3 fusion.113
  545.2 16.1 %all-gather.20.cloned.1.call-done = bf16[96,64,128]{2,1,0:T(8,128)(2,1)} async-done(((bf16[24,64,128]{2,1,0:T(8,128)(2,1)}), bf16[96,64,128]{2,1,0:T(8,128)(2,1)}) %all-gather.20.cloned.1.call-update) | async-done | bytes 1572880 | tf_op jit(solution)/shard_map/all_gather | solution.py:58
  561.3 5.3 while.69
  569.2 3.3 fusion.92
  572.5 7.3 multiply_reduce_fusion.6
  579.8 3.2 copy.327
  584.7 3.9 multiply_reduce_fusion.2
  615.6 5.8 convolution_convert_fusion
  621.4 7.1 fusion.99
  629.4 7.3 pad_maximum_fusion.2
  636.6 11.9 %copy.352 = bf16[1024,4133]{1,0:T(8,128)(2,1)} copy(bf16[1024,4133]{0,1:T(8,128)(2,1)} %pad_maximum_fusion.2) | data formatting | bytes 16928768
  649.9 4.7 fusion.83
  654.6 41.5 %psum.7 = f32[3,24]{1,0:T(4,128)S(1)} all-reduce(f32[3,24]{1,0:T(4,128)S(1)} %add_add_fusion.5), channel_id=1, replica_groups=mesh['batch'=8,'seq'=4] {'batch','seq'}, use_global_device_ids=true, to_apply=%region_48.49 | all-reduce | flops 72 | bytes 576 | tf_op jit(solution)/shard_map/psum | solution.py:478
  699.6 83.0 %reduce-scatter.10.cloned.1.call-done = bf16[32,4133]{1,0:T(8,128)(2,1)} async-done(((bf16[1024,4133]{1,0:T(8,128)(2,1)}), bf16[32,4133]{1,0:T(8,128)(2,1)}) %reduce-scatter.10.cloned.1.call-update) | async-done | bytes 264528 | tf_op jit(solution)/shard_map/reduce_scatter | solution.py:473
  785.9 2.8 multiply_subtract_fusion
  788.6 178.3 %reduce-scatter.8.cloned.1.call-done = bf16[32,8192]{1,0:T(8,128)(2,1)} async-done(((bf16[1024,8192]{1,0:T(8,128)(2,1)}), bf16[32,8192]{1,0:T(8,128)(2,1)}) %reduce-scatter.8.cloned.1.call-update) | async-done | bytes 524304 | tf_op jit(solution)/shard_map/reduce_scatter | solution.py:381
  (445 shorter events, 127.4 us)
Async XLA Ops:
  7.2 85.5 %all-gather.10.cloned.1.call-start = ((), (), s32[]{:S(2)}) async-start(), calls=%async_computation.3 | async-start | bytes 8921088 | tf_op jit(solution)/shard_map/all_gather | solution.py:235
  10.8 160.0 %all-gather.18.cloned.1.call-start = ((), (), s32[]{:S(2)}) async-start(), calls=%async_computation.9 | async-start | bytes 1966080 | tf_op jit(solution)/shard_map/all_gather | solution.py:38
  11.1 90.5 %copy-start.84 = (f32[256]{0:T(256)}, f32[256]{0:T(256)S(1)}, u32[]{:S(2)}) copy-start(f32[256]{0:T(256)S(1)} %fusion.162) | copy-start | bytes 3076
  11.6 94.6 %copy-start.97 = (f32[24]{0:T(128)}, f32[24]{0:T(128)S(1)}, u32[]{:S(2)}) copy-start(f32[24]{0:T(128)S(1)} %get-tuple-element.737) | copy-start | bytes 292
  11.6 94.6 %copy-start.98 = (f32[24]{0:T(128)}, f32[24]{0:T(128)S(1)}, u32[]{:S(2)}) copy-start(f32[24]{0:T(128)S(1)} %get-tuple-element.738) | copy-start | bytes 292
  104.0 7.6 collective-permute-start
  107.3 21.9 %copy-start.63 = (f32[256,24]{0,1:T(8,128)}, f32[256,24]{0,1:T(8,128)S(1)}, u32[]{:S(2)}) copy-start(f32[256,24]{0,1:T(8,128)S(1)} %bitcast_bitcast_fusion) | copy-start | bytes 73732
  107.6 14.6 %copy-start.42 = (f32[256,24]{0,1:T(8,128)}, f32[256,24]{0,1:T(8,128)S(1)}, u32[]{:S(2)}) copy-start(f32[256,24]{0,1:T(8,128)S(1)} %get-tuple-element.733) | copy-start | bytes 73732
  107.6 64.9 %copy-start.59 = (f32[256,24]{0,1:T(8,128)}, f32[256,24]{0,1:T(8,128)S(1)}, u32[]{:S(2)}) copy-start(f32[256,24]{0,1:T(8,128)S(1)} %get-tuple-element.732) | copy-start | bytes 73732
  111.6 60.9 %copy-start.56 = (f32[256,24]{0,1:T(8,128)}, f32[256,24]{0,1:T(8,128)S(1)}, u32[]{:S(2)}) copy-start(f32[256,24]{0,1:T(8,128)S(1)} %copy.311) | copy-start | bytes 73732
  117.7 53.3 %copy-start.7 = (f32[256,1792]{1,0:T(8,128)}, f32[256,1792]{1,0:T(8,128)S(1)}, u32[]{:S(2)}) copy-start(f32[256,1792]{1,0:T(8,128)S(1)} %get-tuple-element.696) | copy-start | bytes 5505028
  125.9 84.7 %all-gather.12.cloned.1.call-start = ((), (), s32[]{:S(2)}) async-start(), calls=%async_computation.4 | async-start | bytes 4325376 | tf_op jit(solution)/shard_map/all_gather | solution.py:241
  126.6 163.3 %all-gather.14.cloned.1.call-start = ((), (), s32[]{:S(2)}) async-start(), calls=%async_computation.5 | async-start | bytes 8650752 | tf_op jit(solution)/shard_map/all_gather | solution.py:242
  127.5 226.4 %all-gather.16.cloned.1.call-start = ((), (), s32[]{:S(2)}) async-start(), calls=%async_computation.6 | async-start | bytes 4325376 | tf_op jit(solution)/shard_map/all_gather | solution.py:243
  128.2 409.5 %reduce-scatter.6.cloned.1.call-start = ((), (), s32[]{:S(2)}) async-start(), calls=%async_computation.7 | async-start | bytes 655360 | tf_op jit(solution)/shard_map/reduce_scatter | solution.py:435
  129.2 10.3 %copy-start.37 = (f32[256,32]{0,1:T(8,128)}, f32[256,32]{0,1:T(8,128)S(1)}, u32[]{:S(2)}) copy-start(f32[256,32]{0,1:T(8,128)S(1)} %get-tuple-element.739) | copy-start | bytes 98308
  129.2 10.3 %copy-start.39 = (f32[256,32]{0,1:T(8,128)}, f32[256,32]{0,1:T(8,128)S(1)}, u32[]{:S(2)}) copy-start(f32[256,32]{0,1:T(8,128)S(1)} %get-tuple-element.740) | copy-start | bytes 98308
  140.7 12.7 %copy-start.78 = (f32[3584]{0:T(1024)S(1)}, f32[3584]{0:T(1024)}, u32[]{:S(2)}) copy-start(f32[3584]{0:T(1024)} %copy-done.77) | copy-start | bytes 43012
  153.4 324.4 %copy-start.61 = (f32[1536]{0:T(1024)}, f32[1536]{0:T(1024)S(1)}, u32[]{:S(2)}) copy-start(f32[1536]{0:T(1024)S(1)} %slice.271) | copy-start | bytes 18436
  183.7 31.7 %copy-start.94 = (f32[256]{0:T(256)}, f32[256]{0:T(256)S(1)}, u32[]{:S(2)}) copy-start(f32[256]{0:T(256)S(1)} %get-tuple-element.694) | copy-start | bytes 3076
  183.7 26.9 %copy-start.55 = (bf16[256,512]{1,0:T(8,128)(2,1)S(1)}, bf16[256,512]{1,0:T(8,128)(2,1)}, u32[]{:S(2)}) copy-start(bf16[256,512]{1,0:T(8,128)(2,1)} %copy.319) | copy-start | bytes 786436
  183.7 294.1 %copy-start.83 = (f32[256]{0:T(256)}, f32[256]{0:T(256)S(1)}, u32[]{:S(2)}) copy-start(f32[256]{0:T(256)S(1)} %fusion.163) | copy-start | bytes 3076
  215.4 189.0 %copy-start.79 = (f32[256]{0:T(256)}, f32[256]{0:T(256)S(1)}, u32[]{:S(2)}) copy-start(f32[256]{0:T(256)S(1)} %fusion.164) | copy-start | bytes 3076
  353.9 17.2 %copy-start.17 = (bf16[256,1024]{1,0:T(8,128)(2,1)S(1)}, bf16[256,1024]{1,0:T(8,128)(2,1)}, u32[]{:S(2)}) copy-start(bf16[256,1024]{1,0:T(8,128)(2,1)} %param.34) | copy-start | bytes 1572868
  372.4 17.8 %copy-start.5 = (f32[256,1024]{1,0:T(8,128)S(1)}, f32[256,1024]{1,0:T(8,128)}, u32[]{:S(2)}) copy-start(f32[256,1024]{1,0:T(8,128)} %get-tuple-element.742) | copy-start | bytes 3145732
  491.9 69.3 %all-gather.20.cloned.1.call-start = ((), (), s32[]{:S(2)}) async-start(), calls=%async_computation.10 | async-start | bytes 1966080 | tf_op jit(solution)/shard_map/all_gather | solution.py:58
  517.4 265.2 %reduce-scatter.10.cloned.1.call-start = ((), (), s32[]{:S(2)}) async-start(), calls=%async_computation.11 | async-start | bytes 8921088 | tf_op jit(solution)/shard_map/reduce_scatter | solution.py:473
  522.7 18.2 %copy-start.62 = (f32[1536]{0:T(1024)S(1)}, f32[1536]{0:T(1024)}, u32[]{:S(2)}) copy-start(f32[1536]{0:T(1024)} %copy-done.61) | copy-start | bytes 18436
  540.9 20.3 %copy-start.106 = (bf16[4,24]{1,0:T(4,128)(2,1)S(1)}, bf16[4,24]{1,0:T(4,128)(2,1)}, u32[]{:S(2)}) copy-start(bf16[4,24]{1,0:T(4,128)(2,1)} %copy-done.105) | copy-start | bytes 580
  561.3 11.2 %copy-start.65 = (f32[256,24]{0,1:T(8,128)S(1)}, f32[256,24]{0,1:T(8,128)}, u32[]{:S(2)}) copy-start(f32[256,24]{0,1:T(8,128)} %copy-done.63) | copy-start | bytes 73732
  561.3 11.2 %copy-start.76 = (pred[256,256]{1,0:T(8,128)(4,1)S(1)}, pred[256,256]{1,0:T(8,128)(4,1)}, u32[]{:S(2)}) copy-start(pred[256,256]{1,0:T(8,128)(4,1)} %iota_compare_fusion) | copy-start | bytes 196612
  593.0 15.6 %copy-start.81 = (f32[1792]{0:T(1024)S(1)}, f32[1792]{0:T(1024)}, u32[]{:S(2)}) copy-start(f32[1792]{0:T(1024)} %get-tuple-element.583) | copy-start | bytes 21508
  593.0 15.6 %copy-start.31 = (f32[256,24]{1,0:T(8,128)S(1)}, f32[256,24]{1,0:T(8,128)}, u32[]{:S(2)}) copy-start(f32[256,24]{1,0:T(8,128)} %copy-done.30) | copy-start | bytes 73732
  593.8 18.9 %collective-permute-start.1 = (f32[3,1792]{1,0:T(4,128)}, f32[3,1792]{1,0:T(4,128)S(1)}, u32[]{:S(2)}, u32[]{:S(2)}) collective-permute-start(f32[3,1792]{1,0:T(4,128)} %pad_add_fusion.1), channel_id=1, source_target_pairs={{1,0},{2,1},{3,2},{5,4},{6,5},{7,6},{9,8},{10,9},{11,10},{13,12},{... | collective-permute-start | bytes 64520 | tf_op jit(solution)/shard_map/ppermute | solution.py:32
  648.6 318.3 %reduce-scatter.8.cloned.1.call-start = ((), (), s32[]{:S(2)}) async-start(), calls=%async_computation.8 | async-start | bytes 17301504 | tf_op jit(solution)/shard_map/reduce_scatter | solution.py:381
  649.8 46.3 %copy-start.102 = (f32[3,24]{1,0:T(4,128)S(1)}, f32[3,24]{1,0:T(4,128)}, u32[]{:S(2)}) copy-start(f32[3,24]{1,0:T(4,128)} %param.55) | copy-start | bytes 868
  649.8 46.3 %copy-start.103 = (f32[3,24]{1,0:T(4,128)S(1)}, f32[3,24]{1,0:T(4,128)}, u32[]{:S(2)}) copy-start(f32[3,24]{1,0:T(4,128)} %param.54) | copy-start | bytes 868
  649.8 46.9 %copy-start.93 = (f32[256]{0:T(256)S(1)}, f32[256]{0:T(256)}, u32[]{:S(2)}) copy-start(f32[256]{0:T(256)} %copy-done.92) | copy-start | bytes 3076
  649.8 46.9 %copy-start.18 = (bf16[256,1024]{1,0:T(8,128)(2,1)S(1)}, bf16[256,1024]{1,0:T(8,128)(2,1)}, u32[]{:S(2)}) copy-start(bf16[256,1024]{1,0:T(8,128)(2,1)} %param.34) | copy-start | bytes 1572868
  649.9 46.9 %copy-start.20 = (f32[256,1024]{1,0:T(8,128)S(1)}, f32[256,1024]{1,0:T(8,128)}, u32[]{:S(2)}) copy-start(f32[256,1024]{1,0:T(8,128)} %copy-done.19) | copy-start | bytes 3145732
  649.9 46.9 %copy-start.80 = (f32[256]{0:T(256)S(1)}, f32[256]{0:T(256)}, u32[]{:S(2)}) copy-start(f32[256]{0:T(256)} %copy-done.79) | copy-start | bytes 3076
  649.9 46.9 %copy-start.90 = (f32[256]{0:T(256)S(1)}, f32[256]{0:T(256)}, u32[]{:S(2)}) copy-start(f32[256]{0:T(256)} %copy-done.89) | copy-start | bytes 3076
  696.8 87.9 %copy-start.108 = (f32[112]{0:T(128)S(1)}, f32[112]{0:T(128)}, u32[]{:S(2)}) copy-start(f32[112]{0:T(128)} %param.39) | copy-start | bytes 1348
  696.8 87.9 %copy-start.109 = (f32[112]{0:T(128)S(1)}, f32[112]{0:T(128)}, u32[]{:S(2)}) copy-start(f32[112]{0:T(128)} %param.51) | copy-start | bytes 1348
  696.8 87.9 %copy-start.110 = (f32[112]{0:T(128)S(1)}, f32[112]{0:T(128)}, u32[]{:S(2)}) copy-start(f32[112]{0:T(128)} %param.50) | copy-start | bytes 1348
  696.8 88.4 %copy-start.88 = (f32[5,56]{1,0:T(8,128)S(1)}, f32[5,56]{1,0:T(8,128)}, u32[]{:S(2)}) copy-start(f32[5,56]{1,0:T(8,128)} %param.40) | copy-start | bytes 3364
  696.8 88.4 %copy-start.99 = (f32[5,56]{1,0:T(8,128)S(1)}, f32[5,56]{1,0:T(8,128)}, u32[]{:S(2)}) copy-start(f32[5,56]{1,0:T(8,128)} %param.53) | copy-start | bytes 3364
  696.8 88.4 %copy-start.100 = (f32[5,56]{1,0:T(8,128)S(1)}, f32[5,56]{1,0:T(8,128)}, u32[]{:S(2)}) copy-start(f32[5,56]{1,0:T(8,128)} %param.52) | copy-start | bytes 3364
  (78 other events, 260.4 us)
Sparse Core Ops, SparseCore 0:
  11.5 81.1 all-gather.9
  126.0 19.7 all-gather.17
  149.2 61.3 all-gather.11
  213.9 75.9 all-gather.13
  293.2 60.6 all-gather.15
  492.1 45.5 reduce-scatter.5
  539.9 21.3 all-gather.19
  648.7 133.8 reduce-scatter.9
  785.0 181.8 reduce-scatter.7

commit v2 on v1

--- a/solution.py
+++ b/solution.py
@@ -154,8 +154,71 @@
     return (earlier[0] * later[0], later[0][:, None, None] * earlier[1] + later[1])
 
 
-def swiglu(gate_up):
-    return jax.nn.silu(gate_up[:, :FF]) * gate_up[:, FF:]
+def swiglu(gate_part, up_part):
+    return jax.nn.silu(gate_part) * up_part
+
+
+def index_bits():
+    found = []
+    for axis in ("seq", "batch"):
+        found += [(axis, 1 << k) for k in range(lax.axis_size(axis).bit_length() - 1)]
+    return found
+
+
+def exchange_orders(bits):
+    along = [bit for bit in bits if bit[0] == "seq"]
+    across = [bit for bit in bits if bit[0] == "batch"]
+    core, xs = along[:1], along[1:]
+    ys, zs, last = across[:-2], across[-2:-1], across[-1:]
+    return core + xs + ys + zs + last, core + ys + zs + xs + last, core + zs + xs + ys + last
+
+
+def swapped(value, bit):
+    axis, mask = bit
+    pairs = [(i, i ^ mask) for i in range(lax.axis_size(axis))]
+    return lax.ppermute(value, axis, pairs)
+
+
+def own_bit(bit):
+    axis, mask = bit
+    return (lax.axis_index(axis) // mask) % 2
+
+
+def gather_rows(block, bits, order):
+    rows, width = block.shape
+    held = []
+    for bit in reversed(order):
+        other = swapped(block, bit)
+        below = sum(1 for b in held if bits.index(b) < bits.index(bit))
+        split = ((1 << (len(held) - below)), (1 << below) * rows, width)
+        mine, theirs = block.reshape(split), other.reshape(split)
+        low = own_bit(bit) == 0
+        block = jnp.stack(
+            [jnp.where(low, mine, theirs), jnp.where(low, theirs, mine)], axis=1
+        ).reshape(-1, width)
+        held.append(bit)
+    return block
+
+
+def scatter_rows(total, bits, order):
+    rows, width = total.shape[0] >> len(bits), total.shape[1]
+    left = list(bits)
+    for bit in order:
+        below = left.index(bit)
+        left.remove(bit)
+        split = total.reshape(1 << (len(left) - below), 2, (1 << below) * rows, width)
+        place = own_bit(bit)
+        keep = lax.dynamic_index_in_dim(split, place, 1, False).reshape(-1, width)
+        send = lax.dynamic_index_in_dim(split, 1 - place, 1, False).reshape(-1, width)
+        got = swapped(send, bit)
+        total = (keep.astype(jnp.float32) + got.astype(jnp.float32)).astype(total.dtype)
+    return total
+
+
+def sum_everywhere(value, bits):
+    for bit in bits:
+        value = value + swapped(value, bit)
+    return value
 
 
 def adamw_update(weight, gradient, moment_one, moment_two, rate, decay):
@@ -175,17 +238,6 @@
     width = -(-vectors.shape[0] // rows)
     vectors = jnp.pad(vectors, (0, width * rows - vectors.shape[0])).reshape(rows, width)
     return jnp.concatenate([weights, vectors], axis=1).astype(jnp.bfloat16)
-
-
-def pack_late(weights, gains, taps, devices):
-    rows = weights.shape[0] // devices
-    split_taps = jnp.transpose(taps.reshape(CONV + 1, devices, -1), (1, 0, 2))
-    vectors = jnp.concatenate([gains.reshape(devices, -1), split_taps.reshape(devices, -1)], axis=1)
-    width = -(-vectors.shape[1] // rows)
-    vectors = jnp.pad(vectors, ((0, 0), (0, width * rows - vectors.shape[1])))
-    return jnp.concatenate([weights, vectors.reshape(devices * rows, width)], axis=1).astype(
-        jnp.bfloat16
-    )
 
 
 def unpack_vectors(packed, start, devices, gains, taps):
@@ -237,11 +289,17 @@
     )
     full_project = full_packed[:, : w_project.shape[1]]
     full_gains, full_conv = unpack_vectors(full_packed, w_project.shape[1], devices, gains, conv_params)
-    full_mixout, full_gateup, full_down = (
-        lax.all_gather(w_mixout.astype(jnp.bfloat16), ("batch", "seq"), axis=0, tiled=True),
-        lax.all_gather(w_gateup.astype(jnp.bfloat16), ("batch", "seq"), axis=0, tiled=True),
-        lax.all_gather(w_down.astype(jnp.bfloat16), ("batch", "seq"), axis=0, tiled=True),
-    )
+    full_pair = lax.all_gather(
+        jnp.concatenate([w_mixout, w_down], axis=0).astype(jnp.bfloat16),
+        ("batch", "seq"),
+        axis=0,
+    )
+    full_mixout = full_pair[:, : 2 * share].reshape(-1, D)
+    full_down = full_pair[:, 2 * share :].reshape(-1, D)
+    bits = index_bits()
+    order_a, order_b, order_c = exchange_orders(bits)
+    full_gate = gather_rows(w_gateup[:, :FF].astype(jnp.bfloat16), bits, order_a)
+    full_up = gather_rows(w_gateup[:, FF:].astype(jnp.bfloat16), bits, order_b)
     gains_f = full_gains.astype(jnp.float32)
     gain_first = gains_f[:D]
     gain_second = gains_f[D : 2 * D]
@@ -267,10 +325,10 @@
     queries = query_rot.astype(jnp.bfloat16).reshape(row_count, KV_HEADS, group_size, HEAD_DIM)
     key_local = key_rot.reshape(row_count, kv_width).astype(jnp.bfloat16)
     value_local = projected[:, q_width + kv_width : offset_cols].astype(jnp.bfloat16)
-    key_all, value_all = (
-        lax.all_gather(key_local, "seq", axis=0, tiled=True),
-        lax.all_gather(value_local, "seq", axis=0, tiled=True),
-    )
+    key_value = lax.all_gather(
+        jnp.concatenate([key_local, value_local], axis=1), "seq", axis=0, tiled=True
+    )
+    key_all, value_all = key_value[:, :kv_width], key_value[:, kv_width:]
 
     def scores_for(key_source, shard):
         key_block = lax.dynamic_slice_in_dim(key_source, shard * row_count, row_count, 0)
@@ -349,36 +407,40 @@
     hidden = tokens_f + jnp.dot(joined, full_mixout, preferred_element_type=jnp.float32)
     normed2_f, pull_second = jax.vjp(rms_scale, hidden, gain_second)
     normed2 = normed2_f.astype(jnp.bfloat16)
-    gate_up = jnp.dot(normed2, full_gateup, preferred_element_type=jnp.float32)
-    swiglu_out, pull_swiglu = jax.vjp(swiglu, gate_up)
+    gate_part = jnp.dot(normed2, full_gate, preferred_element_type=jnp.float32)
+    up_part = jnp.dot(normed2, full_up, preferred_element_type=jnp.float32)
+    swiglu_out, pull_swiglu = jax.vjp(swiglu, gate_part, up_part)
     activated = swiglu_out.astype(jnp.bfloat16)
     out_block = (hidden + jnp.dot(activated, full_down, preferred_element_type=jnp.float32)).astype(
         jnp.bfloat16
     )
-    back_project, back_mixout, back_gateup, back_down = (
+    back_project, back_mixout, back_down = (
         full_project,
         full_mixout,
-        full_gateup,
         full_down,
     )
     grad_out = cotangent.astype(jnp.float32)
     grad_down = jnp.einsum("tf,td->fd", activated, cotangent, preferred_element_type=jnp.float32)
     grad_act = jnp.einsum("td,fd->tf", cotangent, back_down, preferred_element_type=jnp.float32)
-    (grad_gu_f,) = pull_swiglu(grad_act)
-    grad_gu = grad_gu_f.astype(jnp.bfloat16)
-    grad_gateup = jnp.einsum("tc,tf->cf", normed2, grad_gu, preferred_element_type=jnp.float32)
-    grad_normed2 = jnp.einsum("tf,cf->tc", grad_gu, back_gateup, preferred_element_type=jnp.float32)
+    grad_gate_f, grad_up_f = pull_swiglu(grad_act)
+    grad_gate_t = grad_gate_f.astype(jnp.bfloat16)
+    grad_up_t = grad_up_f.astype(jnp.bfloat16)
+    grad_gate = jnp.einsum("tc,tf->cf", normed2, grad_gate_t, preferred_element_type=jnp.float32)
+    grad_up = jnp.einsum("tc,tf->cf", normed2, grad_up_t, preferred_element_type=jnp.float32)
+    grad_normed2 = jnp.einsum(
+        "tf,cf->tc", grad_gate_t, full_gate, preferred_element_type=jnp.float32
+    ) + jnp.einsum("tf,cf->tc", grad_up_t, full_up, preferred_element_type=jnp.float32)
     grad_hidden_n, grad_gain_second = pull_second(grad_normed2)
     grad_hidden = grad_out + grad_hidden_n
     grad_branch = grad_hidden.astype(jnp.bfloat16)
     grad_mixout = jnp.einsum("tr,td->rd", joined, grad_branch, preferred_element_type=jnp.float32)
-    pair = jnp.stack([grad_mixout, grad_down], axis=0).astype(jnp.bfloat16)
-    pair = jnp.transpose(pair.reshape(2, devices, 2, share, D), (1, 3, 2, 0, 4))
-    early = jnp.concatenate(
-        [grad_gateup.astype(jnp.bfloat16), pair.reshape(devices * share, 4 * D)], axis=1
-    )
+    early = tuple(g.astype(jnp.bfloat16) for g in (grad_down, grad_mixout, grad_gate, grad_up))
     early, grad_branch = lax.optimization_barrier((early, grad_branch))
-    own_early = lax.psum_scatter(early, ("batch", "seq"), scatter_dimension=0, tiled=True)
+    own_down = scatter_rows(early[0], bits, order_a).astype(jnp.float32)
+    own_mixout = scatter_rows(early[1], bits, order_b).astype(jnp.float32)
+    own_gate = scatter_rows(early[2], bits, order_c).astype(jnp.float32)
+    own_up = scatter_rows(early[3], bits, order_a).astype(jnp.float32)
+    own_gateup = jnp.concatenate([own_gate, own_up], axis=1)
     grad_joined = jnp.einsum(
         "td,rd->tr", grad_branch, back_mixout, preferred_element_type=jnp.float32
     )
@@ -460,27 +522,35 @@
     grad_projected = jnp.concatenate(
         [grad_query_pre, grad_key_pre, grad_kv_own[:, kv_width:], g_gate_z, g_xbc, g_dtraw], axis=1
     ).astype(jnp.bfloat16)
+    half_cols = offset_cols + inner_width
     grad_project = jnp.einsum(
         "tc,tk->ck", normed, grad_projected, preferred_element_type=jnp.float32
-    )
+    ).astype(jnp.bfloat16)
+    grad_left, grad_right = grad_project[:, :half_cols], grad_project[:, half_cols:]
     grad_normed = jnp.einsum(
         "tk,ck->tc", grad_projected, back_project, preferred_element_type=jnp.float32
     )
     grad_tokens_n, grad_gain_first = pull_first(grad_normed)
     grad_tokens = grad_hidden + grad_tokens_n
     grad_gains = jnp.concatenate([grad_gain_first, grad_gain_second, g_gain_mamba], axis=0)
-    late = pack_late(grad_project, grad_gains, g_conv, devices)
-    own_late = lax.psum_scatter(late, ("batch", "seq"), scatter_dimension=0, tiled=True).astype(
-        jnp.float32
-    )
-    own_project = own_late[:, : w_project.shape[1]]
-    own_gains, own_conv = unpack_vectors(own_late, w_project.shape[1], 1, gains, conv_params)
-    grad_head = lax.psum(g_head_out + g_head_prep, ("batch", "seq"))
-    own_early = own_early.astype(jnp.float32)
-    own_gateup = own_early[:, : 2 * FF]
-    own_pair = own_early[:, 2 * FF :].reshape(share, 2, 2, D)
-    own_pair = jnp.transpose(own_pair, (2, 1, 0, 3)).reshape(2, 2 * share, D)
-    own_mixout, own_down = own_pair[0], own_pair[1]
+    own_left = scatter_rows(grad_left.astype(jnp.bfloat16), bits, order_b)
+    own_right = scatter_rows(grad_right.astype(jnp.bfloat16), bits, order_c)
+    own_project = jnp.concatenate([own_left, own_right], axis=1).astype(jnp.float32)
+    head_part = g_head_out + g_head_prep
+    vectors = jnp.concatenate([grad_gains, g_conv.reshape(-1), head_part.reshape(-1)])
+    vectors = jnp.pad(vectors, (0, -vectors.shape[0] % 1024)).reshape(-1, 128)
+    vectors = sum_everywhere(vectors, bits).reshape(-1)
+    place = lax.axis_index("batch") * lax.axis_size("seq") + lax.axis_index("seq")
+    gain_count, tap_count = grad_gains.shape[0], g_conv.size
+    own_gains = lax.dynamic_slice_in_dim(vectors, place * gains.shape[0], gains.shape[0])
+    own_conv = lax.dynamic_slice_in_dim(
+        vectors[gain_count : gain_count + tap_count].reshape(g_conv.shape),
+        place * conv_params.shape[1],
+        conv_params.shape[1],
+        1,
+    )
+    grad_head = vectors[gain_count + tap_count : gain_count + tap_count + head_part.size]
+    grad_head = grad_head.reshape(head_part.shape)
     r_project = adamw_update(
         w_project, own_project, mom_project, sec_project, rate_matrix, weight_decay
     )

time: 988 us -> 700 us (0.71)
  waiting for transfers between devices: 524 us -> 241 us
  starting transfers between devices: 4.03 us -> 73.8 us
  blocking collectives: 63.8 us -> 14.8 us
  matrix products: 132 us -> 100 us
  local copies, waits for them, and re-layouts: 125 us -> 137 us
  other arithmetic: 114 us -> 104 us
    reduce_scatter x2 -> x0, waiting for transfers between devices: 261 us -> none  [the longest x1 178 us: local(): lax.psum_scatter(early, ('batch', 'seq'), scatter_dimension=0, tiled=True)]
    all_gather x3 -> x1, waiting for transfers between devices: 156 us -> 0.01 us  [local(): lax.all_gather(jnp.concatenate([w_mixout, w_down], axis=0).astype(jnp.bfl...]
    ppermute x0 -> x45, waiting for transfers between devices: none -> 156 us  [swapped(): return lax.ppermute(value, axis, pairs)]
    ppermute x0 -> x45, starting transfers between devices: none -> 69.3 us  [swapped(): return lax.ppermute(value, axis, pairs)]
    psum x1 -> x0, blocking collectives: 41.5 us -> none  [local(): grad_head = lax.psum(g_head_out + g_head_prep, ('batch', 'seq'))]
    dynamic_slice x0 -> x24, local copies, waits for them, and re-layouts: none -> 30.9 us  [scatter_rows(): keep = lax.dynamic_index_in_dim(split, place, 1, False).reshape(-1, width)]
    another operation x10 -> x14, local copies, waits for them, and re-layouts: 37.5 us -> 7.25 us  [the longest x7 6.18 us: gather_rows(): jnp.stack([jnp.where(low, mine, theirs), jnp.where(low, theirs, mine)], a...]
    slice x6 -> x10, local copies, waits for them, and re-layouts: 1.81 us -> 26.9 us  [the longest x2 10.4 us: local(): grad_project[:, half_cols:]]
  transfers between devices with their start and end apart: 11 -> 52, of which waited for: 8 -> 25; matrix products, arithmetic and copies ran while one was open for 13% -> 35% of each run, Pallas kernels for 0% -> 0%
where the time goes in v2:
time: 700 us; the launch traced here: 688 us
  waiting for transfers between devices  241 us (34%)
  local copies, waits for them, and re-layouts  137 us (20%)
  other arithmetic  104 us (15%)
  matrix products  100 us (14%)
  starting transfers between devices  73.8 us (11%)
  between operations  16.8 us (2%)
  blocking collectives  14.8 us (2%)
    ppermute x45, waiting for transfers between devices, swapped(): return lax.ppermute(value, axis, pairs)  156 us
    all_gather x1, waiting for transfers between devices, local(): lax.all_gather(pack_project(w_project, gains, conv_params), ('batch', 'se...  73.6 us
    ppermute x45, starting transfers between devices, swapped(): return lax.ppermute(value, axis, pairs)  69.3 us
    dynamic_slice x24, local copies, waits for them, and re-layouts, scatter_rows(): keep = lax.dynamic_index_in_dim(split, place, 1, False).reshape(-1, width)  30.9 us
    dot_general x3, matrix products, mamba_output(): within = jnp.einsum('tsh,shp->thp', mixing, inputs, precision=highest)  25.7 us
    convert_element_type x28, other arithmetic, scatter_rows(): (keep.astype(jnp.float32) + got.astype(jnp.float32)).astype(total.dtype)  25 us
    unnamed x277, local copies, waits for them, and re-layouts  24.2 us
  transfers between devices with their start and end apart: 52, of which 25 were waited for; matrix products, arithmetic and copies ran while one was open for 35% of the time, Pallas kernels for 0%

profile of v2, /device:TPU:0, one launch (start us, length us, event | category | flops | bytes accessed | tf_op | source)
XLA Modules:
  0.0 688.4 jit_solution(18416218706307473471)
XLA Ops:
  12.8 4.1 collective-permute-start.1
  16.9 6.3 collective-permute-done.1
  23.4 4.1 collective-permute-start.2
  27.5 9.0 %collective-permute-done.6 = bf16[32,2048]{1,0:T(8,128)(2,1)S(1)} collective-permute-done((bf16[32,2048]{1,0:T(8,128)(2,1)S(1)}, bf16[32,2048]{1,0:T(8,128)(2,1)S(1)}, u32[]{:S(2)}, u32[]{:S(2)}) %collective-permute-start.6) | collective-permute-done | bytes 131104 | tf_op jit(solution)/shard_map/ppermute | solution.py:179
  44.0 13.1 %collective-permute-done.3 = bf16[128,2048]{1,0:T(8,128)(2,1)S(1)} collective-permute-done((bf16[128,2048]{1,0:T(8,128)(2,1)S(1)}, bf16[128,2048]{1,0:T(8,128)(2,1)S(1)}, u32[]{:S(2)}, u32[]{:S(2)}) %collective-permute-start.3) | collective-permute-done | bytes 524320 | tf_op jit(solution)/shard_map/ppermute | solution.py:179
  59.0 8.1 %collective-permute-done.8 = bf16[128,2048]{1,0:T(8,128)(2,1)S(1)} collective-permute-done((bf16[128,2048]{1,0:T(8,128)(2,1)S(1)}, bf16[128,2048]{1,0:T(8,128)(2,1)S(1)}, u32[]{:S(2)}, u32[]{:S(2)}) %collective-permute-start.8) | collective-permute-done | bytes 524320 | tf_op jit(solution)/shard_map/ppermute | solution.py:179
  68.3 22.8 %collective-permute-done.4 = bf16[256,2048]{1,0:T(8,128)(2,1)S(1)} collective-permute-done((bf16[256,2048]{1,0:T(8,128)(2,1)S(1)}, bf16[256,2048]{1,0:T(8,128)(2,1)S(1)}, u32[]{:S(2)}, u32[]{:S(2)}) %collective-permute-start.4) | collective-permute-done | bytes 1048608 | tf_op jit(solution)/shard_map/ppermute | solution.py:179
  91.8 13.4 %collective-permute-done.9 = bf16[256,2048]{1,0:T(8,128)(2,1)} collective-permute-done((bf16[256,2048]{1,0:T(8,128)(2,1)}, bf16[256,2048]{1,0:T(8,128)(2,1)}, u32[]{:S(2)}, u32[]{:S(2)}) %collective-permute-start.9) | collective-permute-done | bytes 1048608 | tf_op jit(solution)/shard_map/ppermute | solution.py:179
  117.4 6.2 fusion.218
  123.6 73.6 %all-gather.8.cloned.1.call-done = bf16[1024,4133]{1,0:T(8,128)(2,1)} async-done(((bf16[32,4133]{1,0:T(8,128)(2,1)}), bf16[1024,4133]{1,0:T(8,128)(2,1)}) %all-gather.8.cloned.1.call-update) | async-done | bytes 8464400 | tf_op jit(solution)/shard_map/all_gather | solution.py:287
  198.8 7.2 %fusion.31 = f32[256,4120]{0,1:T(8,128)S(1)} fusion(bf16[1024,4133]{1,0:T(8,128)(2,1)} %all-gather.8.cloned.1.call-done, bf16[256,1024]{1,0:T(8,128)(2,1)S(1)} %copy-done.26, f32[1024]{0:T(1024)S(1)} %get-tuple-element.697, f32[256]{0:T(256)S(1)} %fusion.190), kind=kOutput, calls=%fused_computation.58 | convolution fusion | flops 2161115136 | bytes 13212672 | tf_op jit(solution)/shard_map/dot_general | solution.py:311
  214.5 7.6 %all_gather.29 = bf16[1024,256]{0,1:T(8,128)(2,1)S(1)} all-gather(bf16[256,256]{0,1:T(8,128)(2,1)S(1)} %pad_maximum_fusion.20), channel_id=1, replica_groups=mesh['batch'=8,'seq'=4] {'seq'}, dimensions={0}, use_global_device_ids=true | all-gather | bytes 655360 | tf_op jit(solution)/shard_map/all_gather | solution.py:328
  230.3 7.1 %all-gather.2 = bf16[4,1,24]{2,1,0:T(2,128)(2,1)S(1)} all-gather(bf16[1,1,24]{2,1,0:T(2,128)(2,1)S(1)} %bitcast.714), channel_id=1, replica_groups=mesh['batch'=8,'seq'=4] {'seq'}, dimensions={0}, use_global_device_ids=true | all-gather | bytes 240 | tf_op jit(solution)/shard_map/all_gather | solution.py:38
  241.1 6.0 fusion.73
  251.7 3.5 fusion.97
  262.4 11.2 %all-gather.12.cloned.1.call-done = bf16[96,64,128]{2,1,0:T(8,128)(2,1)} async-done(((bf16[24,64,128]{2,1,0:T(8,128)(2,1)}), bf16[96,64,128]{2,1,0:T(8,128)(2,1)}) %all-gather.12.cloned.1.call-update) | async-done | bytes 1572880 | tf_op jit(solution)/shard_map/all_gather | solution.py:38
  275.7 7.0 %fusion.77 = f32[256,24,64]{0,2,1:T(8,128)S(1)} fusion(f32[256,24,64]{0,2,1:T(8,128)S(1)} %bitcast.605, f32[256,24,64]{0,2,1:T(8,128)S(1)} %fusion.166, f32[256,24]{0,1:T(8,128)S(1)} %copy-done.84, f32[256,256]{1,0:T(8,128)S(1)} %copy-done.71, pred[256,256]{1,0:T(8,128)(4,1)S(1)} %copy-done.103, f32[24]{0:T(128)S(1)} %copy-done.132, ...), kind=kOutput, calls=%fused_computation.155 | convolution fusion | flops 1214644224 | bytes 5120096 | tf_op jit(solution)/shard_map/jvp(tsh,shp->thp)/dot_general | solution.py:143
  322.1 8.7 %while.68 = (s32[]{:T(128)}, f32[256,2,4,64]{0,3,2,1:T(8,128)}, bf16[1024,256]{1,0:T(8,128)(2,1)}, s32[]{:T(128)}, bf16[1024,128]{0,1:T(8,128)(2,1)}, /*index=5*...) while((s32[]{:T(128)}, f32[256,2,4,64]{0,3,2,1:T(8,128)}, ...), condition=%wide.region_16.17_spmd.clone, body=%wide.region_15.16_spmd.clone.sunk | while | flops 340460032 | bytes 14110959 | solution.py:488
  333.0 4.4 multiply_reduce_fusion.4
  340.4 4.0 fusion.109
  344.4 5.1 constant_dynamic-slice_fusion.37
  349.5 10.0 %collective-permute-start.22 = (bf16[1024,1024]{1,0:T(8,128)(2,1)}, bf16[1024,1024]{1,0:T(8,128)(2,1)}, u32[]{:S(2)}, u32[]{:S(2)}) collective-permute-start(bf16[1024,1024]{1,0:T(8,128)(2,1)} %bitcast.111), channel_id=1, source_target_pairs={{0,1},{1,0},{2,3},{3,2},{4,5},{5,4},{6,7},{7,6},{8,9},{9,8},{10,11... | collective-permute-start | bytes 6291464 | tf_op jit(solution)/shard_map/ppermute | solution.py:179
  370.8 3.6 fusion.100
  374.4 11.4 %fusion.47 = (f32[256,24]{0,1:T(8,128)}, f32[256,24]{0,1:T(8,128)}, f32[256,256]{1,0:T(8,128)S(1)}) fusion(f32[256,24]{0,1:T(8,128)} %copy-done.83, f32[256,256]{1,0:T(8,128)} %fusion.171, pred[256,256]{1,0:T(8,128)(4,1)} %iota_compare_fusion, f32[24,64,256]{2,1,0:T(8,128)} %bitcast.610, f32[256,24,64]{0,2,1:T(8,128)} %bitcast.604, f32[256,24]{0,1:T(8,128)} %copy-done.78), kind=kOutput, calls=%fused_computation.82 | convolution fusion | flops 1222430720 | bytes 3833856 | tf_op jit(solution)/shard_map/transpose(jvp(tsh,shp->thp))/dot_general | solution.py:143
  389.3 4.9 fusion.96
  397.4 4.4 fusion.132
  411.4 20.1 %collective-permute-start.33 = (bf16[256,2048]{1,0:T(8,128)(2,1)}, bf16[256,2048]{1,0:T(8,128)(2,1)}, u32[]{:S(2)}, u32[]{:S(2)}) collective-permute-start(bf16[256,2048]{1,0:T(8,128)(2,1)} %bitcast.144), channel_id=1, source_target_pairs={{0,2},{1,3},{2,0},{3,1},{4,6},{5,7},{6,4},{7,5},{8,10},{9,11},{10,... | collective-permute-start | bytes 3145736 | tf_op jit(solution)/shard_map/ppermute | solution.py:179
  442.0 5.1 while.69
  453.0 7.3 %multiply_reduce_fusion.6 = (f32[256,24]{0,1:T(8,128)}, f32[256,24]{0,1:T(8,128)}, f32[256,24,64]{0,2,1:T(8,128)}, f32[256,24]{0,1:T(8,128)}) fusion(f32[256,24,64]{0,2,1:T(8,128)S(1)} %fusion.162, f32[256,24,64]{0,2,1:T(8,128)S(1)} %bitcast.607, f32[256,24]{0,1:T(8,128)S(1)} %copy-done.80, f32[256,24,64]{0,2,1:T(8,128)S(1)} %bitcast.611, ...), kind=kOutput, calls=%fused_computation.159 | convolution fusion | flops 1217378304 | bytes 9912416 | tf_op jit(solution)/shard_map/transpose(jvp(tsh,shp->thp))/dot_general | solution.py:143
  465.2 3.9 multiply_reduce_fusion.2
  494.1 5.3 fusion.113
  509.1 6.8 copy.436
  517.2 4.2 constant_dynamic-slice_fusion.53
  528.1 4.4 slice.288
  532.5 6.1 copy.437
  541.8 4.4 constant_dynamic-slice_fusion.45
  546.1 4.3 copy.438
  566.7 5.5 collective-permute-done.24
  579.6 6.7 collective-permute-done.39
  589.3 4.3 collective-permute-done.30
  594.2 3.5 collective-permute-done.40
  598.9 8.4 %collective-permute-done.36 = bf16[32,2048]{1,0:T(8,128)(2,1)S(1)} collective-permute-done((bf16[32,2048]{1,0:T(8,128)(2,1)S(1)}, bf16[32,2048]{1,0:T(8,128)(2,1)S(1)}, u32[]{:S(2)}, u32[]{:S(2)}) %collective-permute-start.36) | collective-permute-done | bytes 131104 | tf_op jit(solution)/shard_map/ppermute | solution.py:179
  611.0 3.9 copy.439
  631.5 11.8 %collective-permute-done.18 = bf16[256,1816]{0,1:T(8,128)(2,1)} collective-permute-done((bf16[256,1816]{0,1:T(8,128)(2,1)}, bf16[256,1816]{0,1:T(8,128)(2,1)}, u32[]{:S(2)}, u32[]{:S(2)}) %collective-permute-start.18) | collective-permute-done | bytes 929824 | tf_op jit(solution)/shard_map/ppermute | solution.py:179
  645.9 6.3 collective-permute-done.13
  657.4 9.2 %collective-permute-done.14 = bf16[128,2304]{1,0:T(8,128)(2,1)S(1)} collective-permute-done((bf16[128,2304]{1,0:T(8,128)(2,1)S(1)}, bf16[128,2304]{1,0:T(8,128)(2,1)S(1)}, u32[]{:S(2)}, u32[]{:S(2)}) %collective-permute-start.14) | collective-permute-done | bytes 589856 | tf_op jit(solution)/shard_map/ppermute | solution.py:179
  667.9 5.8 collective-permute-done.15
  674.0 6.0 collective-permute-done.16
  (655 shorter events, 279.3 us)
Async XLA Ops:
  7.2 110.2 %all-gather.10.cloned.1.call-start = ((), (), s32[]{:S(2)}) async-start(), calls=%async_computation.2 | async-start | bytes 8650752 | tf_op jit(solution)/shard_map/all_gather | solution.py:292
  9.1 188.1 %all-gather.8.cloned.1.call-start = ((), (), s32[]{:S(2)}) async-start(), calls=%async_computation.1 | async-start | bytes 8921088 | tf_op jit(solution)/shard_map/all_gather | solution.py:287
  12.7 260.9 %all-gather.12.cloned.1.call-start = ((), (), s32[]{:S(2)}) async-start(), calls=%async_computation.4 | async-start | bytes 1966080 | tf_op jit(solution)/shard_map/all_gather | solution.py:38
  12.8 10.4 %collective-permute-start.1 = (bf16[32,2048]{1,0:T(8,128)(2,1)S(1)}, bf16[32,2048]{1,0:T(8,128)(2,1)S(1)}, u32[]{:S(2)}, u32[]{:S(2)}) collective-permute-start(bf16[32,2048]{1,0:T(8,128)(2,1)S(1)} %slice.277), channel_id=1, source_target_pairs={{0,16},{4,20},{8,24},{12,28},{16,0},{20,4},{24,8},{28,12},{1,17},{... | collective-permute-start | bytes 393224 | tf_op jit(solution)/shard_map/ppermute | solution.py:179
  23.2 13.2 %collective-permute-start.6 = (bf16[32,2048]{1,0:T(8,128)(2,1)S(1)}, bf16[32,2048]{1,0:T(8,128)(2,1)S(1)}, u32[]{:S(2)}, u32[]{:S(2)}) collective-permute-start(bf16[32,2048]{1,0:T(8,128)(2,1)S(1)} %get-tuple-element.687), channel_id=1, source_target_pairs={{0,16},{4,20},{8,24},{12,28},{16,0},{20,4},{24,8},{28,12},{1,17},{... | collective-permute-start | bytes 393224 | tf_op jit(solution)/shard_map/ppermute | solution.py:179
  23.4 16.4 %collective-permute-start.2 = (bf16[64,2048]{1,0:T(8,128)(2,1)S(1)}, bf16[64,2048]{1,0:T(8,128)(2,1)S(1)}, u32[]{:S(2)}, u32[]{:S(2)}) collective-permute-start(bf16[64,2048]{1,0:T(8,128)(2,1)S(1)} %bitcast.704), channel_id=1, source_target_pairs={{0,8},{4,12},{8,0},{12,4},{16,24},{20,28},{24,16},{28,20},{1,9},{5... | collective-permute-start | bytes 786440 | tf_op jit(solution)/shard_map/ppermute | solution.py:179
  36.5 7.2 %collective-permute-start.7 = (bf16[64,2048]{1,0:T(8,128)(2,1)S(1)}, bf16[64,2048]{1,0:T(8,128)(2,1)S(1)}, u32[]{:S(2)}, u32[]{:S(2)}) collective-permute-start(bf16[64,2048]{1,0:T(8,128)(2,1)S(1)} %bitcast.703), channel_id=1, source_target_pairs={{0,2},{1,3},{2,0},{3,1},{4,6},{5,7},{6,4},{7,5},{8,10},{9,11},{10,... | collective-permute-start | bytes 786440 | tf_op jit(solution)/shard_map/ppermute | solution.py:179
  39.9 17.2 %collective-permute-start.3 = (bf16[128,2048]{1,0:T(8,128)(2,1)S(1)}, bf16[128,2048]{1,0:T(8,128)(2,1)S(1)}, u32[]{:S(2)}, u32[]{:S(2)}) collective-permute-start(bf16[128,2048]{1,0:T(8,128)(2,1)S(1)} %bitcast.653), channel_id=1, source_target_pairs={{0,4},{4,0},{8,12},{12,8},{16,20},{20,16},{24,28},{28,24},{1,5},{5... | collective-permute-start | bytes 1572872 | tf_op jit(solution)/shard_map/ppermute | solution.py:179
  43.9 23.1 %collective-permute-start.8 = (bf16[128,2048]{1,0:T(8,128)(2,1)S(1)}, bf16[128,2048]{1,0:T(8,128)(2,1)S(1)}, u32[]{:S(2)}, u32[]{:S(2)}) collective-permute-start(bf16[128,2048]{1,0:T(8,128)(2,1)S(1)} %bitcast.654), channel_id=1, source_target_pairs={{0,8},{4,12},{8,0},{12,4},{16,24},{20,28},{24,16},{28,20},{1,9},{5... | collective-permute-start | bytes 1572872 | tf_op jit(solution)/shard_map/ppermute | solution.py:179
  57.3 33.8 %collective-permute-start.4 = (bf16[256,2048]{1,0:T(8,128)(2,1)S(1)}, bf16[256,2048]{1,0:T(8,128)(2,1)S(1)}, u32[]{:S(2)}, u32[]{:S(2)}) collective-permute-start(bf16[256,2048]{1,0:T(8,128)(2,1)S(1)} %bitcast.630), channel_id=1, source_target_pairs={{0,2},{1,3},{2,0},{3,1},{4,6},{5,7},{6,4},{7,5},{8,10},{9,11},{10,... | collective-permute-start | bytes 3145736 | tf_op jit(solution)/shard_map/ppermute | solution.py:179
  68.3 36.9 %collective-permute-start.9 = (bf16[256,2048]{1,0:T(8,128)(2,1)}, bf16[256,2048]{1,0:T(8,128)(2,1)}, u32[]{:S(2)}, u32[]{:S(2)}) collective-permute-start(bf16[256,2048]{1,0:T(8,128)(2,1)} %bitcast.48), channel_id=1, source_target_pairs={{0,4},{4,0},{8,12},{12,8},{16,20},{20,16},{24,28},{28,24},{1,5},{5... | collective-permute-start | bytes 3145736 | tf_op jit(solution)/shard_map/ppermute | solution.py:179
  91.7 18.0 %collective-permute-start.5 = (bf16[512,2048]{1,0:T(8,128)(2,1)S(1)}, bf16[512,2048]{1,0:T(8,128)(2,1)}, u32[]{:S(2)}, u32[]{:S(2)}) collective-permute-start(bf16[512,2048]{1,0:T(8,128)(2,1)S(1)} %bitcast.618), channel_id=1, source_target_pairs={{0,1},{1,0},{2,3},{3,2},{4,5},{5,4},{6,7},{7,6},{8,9},{9,8},{10,11... | collective-permute-start | bytes 6291464 | tf_op jit(solution)/shard_map/ppermute | solution.py:179
  107.3 7.1 %collective-permute-start.10 = (bf16[512,2048]{1,0:T(8,128)(2,1)S(1)}, bf16[512,2048]{1,0:T(8,128)(2,1)S(1)}, u32[]{:S(2)}, u32[]{:S(2)}) collective-permute-start(bf16[512,2048]{1,0:T(8,128)(2,1)S(1)} %bitcast.619), channel_id=1, source_target_pairs={{0,1},{1,0},{2,3},{3,2},{4,5},{5,4},{6,7},{7,6},{8,9},{9,8},{10,11... | collective-permute-start | bytes 6291464 | tf_op jit(solution)/shard_map/ppermute | solution.py:179
  209.4 31.6 %collective-permute-start = (f32[3,1792]{1,0:T(4,128)S(1)}, f32[3,1792]{1,0:T(4,128)}, u32[]{:S(2)}, u32[]{:S(2)}) collective-permute-start(f32[3,1792]{1,0:T(4,128)S(1)} %copy.401), channel_id=1, source_target_pairs={{0,1},{1,2},{2,3},{4,5},{5,6},{6,7},{8,9},{9,10},{10,11},{12,13},{... | collective-permute-start | bytes 64520 | tf_op jit(solution)/shard_map/ppermute | solution.py:32
  255.2 138.9 %reduce-scatter.2.cloned.1.call-start = ((), (), s32[]{:S(2)}) async-start(), calls=%async_computation.3 | async-start | bytes 655360 | tf_op jit(solution)/shard_map/reduce_scatter | solution.py:497
  332.9 109.1 %all-gather.14.cloned.1.call-start = ((), (), s32[]{:S(2)}) async-start(), calls=%async_computation.5 | async-start | bytes 1966080 | tf_op jit(solution)/shard_map/all_gather | solution.py:58
  349.5 52.3 %collective-permute-start.22 = (bf16[1024,1024]{1,0:T(8,128)(2,1)}, bf16[1024,1024]{1,0:T(8,128)(2,1)}, u32[]{:S(2)}, u32[]{:S(2)}) collective-permute-start(bf16[1024,1024]{1,0:T(8,128)(2,1)} %bitcast.111), channel_id=1, source_target_pairs={{0,1},{1,0},{2,3},{3,2},{4,5},{5,4},{6,7},{7,6},{8,9},{9,8},{10,11... | collective-permute-start | bytes 6291464 | tf_op jit(solution)/shard_map/ppermute | solution.py:179
  362.1 45.4 %collective-permute-start.32 = (bf16[512,2048]{1,0:T(8,128)(2,1)}, bf16[512,2048]{1,0:T(8,128)(2,1)}, u32[]{:S(2)}, u32[]{:S(2)}) collective-permute-start(bf16[512,2048]{1,0:T(8,128)(2,1)} %bitcast.141), channel_id=1, source_target_pairs={{0,1},{1,0},{2,3},{3,2},{4,5},{5,4},{6,7},{7,6},{8,9},{9,8},{10,11... | collective-permute-start | bytes 6291464 | tf_op jit(solution)/shard_map/ppermute | solution.py:179
  365.8 65.7 %collective-permute-start.27 = (bf16[512,2048]{1,0:T(8,128)(2,1)}, bf16[512,2048]{1,0:T(8,128)(2,1)}, u32[]{:S(2)}, u32[]{:S(2)}) collective-permute-start(bf16[512,2048]{1,0:T(8,128)(2,1)} %bitcast.126), channel_id=1, source_target_pairs={{0,1},{1,0},{2,3},{3,2},{4,5},{5,4},{6,7},{7,6},{8,9},{9,8},{10,11... | collective-permute-start | bytes 6291464 | tf_op jit(solution)/shard_map/ppermute | solution.py:179
  369.4 67.6 %collective-permute-start.37 = (bf16[1024,1024]{1,0:T(8,128)(2,1)}, bf16[1024,1024]{1,0:T(8,128)(2,1)}, u32[]{:S(2)}, u32[]{:S(2)}) collective-permute-start(bf16[1024,1024]{1,0:T(8,128)(2,1)} %bitcast.156), channel_id=1, source_target_pairs={{0,1},{1,0},{2,3},{3,2},{4,5},{5,4},{6,7},{7,6},{8,9},{9,8},{10,11... | collective-permute-start | bytes 6291464 | tf_op jit(solution)/shard_map/ppermute | solution.py:179
  406.0 150.0 %collective-permute-start.23 = (bf16[512,1024]{1,0:T(8,128)(2,1)}, bf16[512,1024]{1,0:T(8,128)(2,1)}, u32[]{:S(2)}, u32[]{:S(2)}) collective-permute-start(bf16[512,1024]{1,0:T(8,128)(2,1)} %bitcast.114), channel_id=1, source_target_pairs={{0,4},{4,0},{8,12},{12,8},{16,20},{20,16},{24,28},{28,24},{1,5},{5... | collective-permute-start | bytes 3145736 | tf_op jit(solution)/shard_map/ppermute | solution.py:179
  411.4 146.9 %collective-permute-start.33 = (bf16[256,2048]{1,0:T(8,128)(2,1)}, bf16[256,2048]{1,0:T(8,128)(2,1)}, u32[]{:S(2)}, u32[]{:S(2)}) collective-permute-start(bf16[256,2048]{1,0:T(8,128)(2,1)} %bitcast.144), channel_id=1, source_target_pairs={{0,2},{1,3},{2,0},{3,1},{4,6},{5,7},{6,4},{7,5},{8,10},{9,11},{10,... | collective-permute-start | bytes 3145736 | tf_op jit(solution)/shard_map/ppermute | solution.py:179
  435.5 126.0 %collective-permute-start.28 = (bf16[256,2048]{1,0:T(8,128)(2,1)}, bf16[256,2048]{1,0:T(8,128)(2,1)}, u32[]{:S(2)}, u32[]{:S(2)}) collective-permute-start(bf16[256,2048]{1,0:T(8,128)(2,1)} %bitcast.129), channel_id=1, source_target_pairs={{0,8},{4,12},{8,0},{12,4},{16,24},{20,28},{24,16},{28,20},{1,9},{5... | collective-permute-start | bytes 3145736 | tf_op jit(solution)/shard_map/ppermute | solution.py:179
  441.1 122.9 %collective-permute-start.38 = (bf16[512,1024]{1,0:T(8,128)(2,1)}, bf16[512,1024]{1,0:T(8,128)(2,1)}, u32[]{:S(2)}, u32[]{:S(2)}) collective-permute-start(bf16[512,1024]{1,0:T(8,128)(2,1)} %bitcast.159), channel_id=1, source_target_pairs={{0,2},{1,3},{2,0},{3,1},{4,6},{5,7},{6,4},{7,5},{8,10},{9,11},{10,... | collective-permute-start | bytes 3145736 | tf_op jit(solution)/shard_map/ppermute | solution.py:179
  474.3 17.8 %collective-permute-start.11 = (f32[3,1792]{1,0:T(4,128)}, f32[3,1792]{1,0:T(4,128)S(1)}, u32[]{:S(2)}, u32[]{:S(2)}) collective-permute-start(f32[3,1792]{1,0:T(4,128)} %pad_add_fusion.2), channel_id=1, source_target_pairs={{1,0},{2,1},{3,2},{5,4},{6,5},{7,6},{9,8},{10,9},{11,10},{13,12},{... | collective-permute-start | bytes 64520 | tf_op jit(solution)/shard_map/ppermute | solution.py:32
  499.5 16.4 %collective-permute-start.42 = (f32[104,128]{1,0:T(8,128)S(1)}, f32[104,128]{1,0:T(8,128)S(1)}, u32[]{:S(2)}, u32[]{:S(2)}) collective-permute-start(f32[104,128]{1,0:T(8,128)S(1)} %pad_bitcast_fusion), channel_id=1, source_target_pairs={{0,1},{1,0},{2,3},{3,2},{4,5},{5,4},{6,7},{7,6},{8,9},{9,8},{10,11... | collective-permute-start | bytes 159752 | tf_op jit(solution)/shard_map/ppermute | solution.py:179
  525.7 12.9 %collective-permute-start.45 = (f32[104,128]{1,0:T(8,128)S(1)}, f32[104,128]{1,0:T(8,128)}, u32[]{:S(2)}, u32[]{:S(2)}) collective-permute-start(f32[104,128]{1,0:T(8,128)S(1)} %add.784), channel_id=1, source_target_pairs={{0,8},{4,12},{8,0},{12,4},{16,24},{20,28},{24,16},{28,20},{1,9},{5... | collective-permute-start | bytes 159752 | tf_op jit(solution)/shard_map/ppermute | solution.py:179
  539.4 11.0 %collective-permute-start.46 = (f32[104,128]{1,0:T(8,128)S(1)}, f32[104,128]{1,0:T(8,128)S(1)}, u32[]{:S(2)}, u32[]{:S(2)}) collective-permute-start(f32[104,128]{1,0:T(8,128)S(1)} %add.785), channel_id=1, source_target_pairs={{0,16},{4,20},{8,24},{12,28},{16,0},{20,4},{24,8},{28,12},{1,17},{... | collective-permute-start | bytes 159752 | tf_op jit(solution)/shard_map/ppermute | solution.py:179
  551.0 60.0 %collective-permute-start.17 = (bf16[512,1816]{0,1:T(8,128)(2,1)}, bf16[512,1816]{0,1:T(8,128)(2,1)}, u32[]{:S(2)}, u32[]{:S(2)}) collective-permute-start(bf16[512,1816]{0,1:T(8,128)(2,1)} %copy.438), channel_id=1, source_target_pairs={{0,1},{1,0},{2,3},{3,2},{4,5},{5,4},{6,7},{7,6},{8,9},{9,8},{10,11... | collective-permute-start | bytes 5578760 | tf_op jit(solution)/shard_map/ppermute | solution.py:179
  556.0 64.9 %collective-permute-start.12 = (bf16[512,2304]{1,0:T(8,128)(2,1)}, bf16[512,2304]{1,0:T(8,128)(2,1)}, u32[]{:S(2)}, u32[]{:S(2)}) collective-permute-start(bf16[512,2304]{1,0:T(8,128)(2,1)} %bitcast.647), channel_id=1, source_target_pairs={{0,1},{1,0},{2,3},{3,2},{4,5},{5,4},{6,7},{7,6},{8,9},{9,8},{10,11... | collective-permute-start | bytes 7077896 | tf_op jit(solution)/shard_map/ppermute | solution.py:179
  558.3 13.9 %collective-permute-start.24 = (bf16[256,1024]{1,0:T(8,128)(2,1)S(1)}, bf16[256,1024]{1,0:T(8,128)(2,1)S(1)}, u32[]{:S(2)}, u32[]{:S(2)}) collective-permute-start(bf16[256,1024]{1,0:T(8,128)(2,1)S(1)} %bitcast.686), channel_id=1, source_target_pairs={{0,8},{4,12},{8,0},{12,4},{16,24},{20,28},{24,16},{28,20},{1,9},{5... | collective-permute-start | bytes 1572872 | tf_op jit(solution)/shard_map/ppermute | solution.py:179
  561.5 14.7 %collective-permute-start.34 = (bf16[128,2048]{1,0:T(8,128)(2,1)S(1)}, bf16[128,2048]{1,0:T(8,128)(2,1)S(1)}, u32[]{:S(2)}, u32[]{:S(2)}) collective-permute-start(bf16[128,2048]{1,0:T(8,128)(2,1)S(1)} %bitcast.687), channel_id=1, source_target_pairs={{0,4},{4,0},{8,12},{12,8},{16,20},{20,16},{24,28},{28,24},{1,5},{5... | collective-permute-start | bytes 1572872 | tf_op jit(solution)/shard_map/ppermute | solution.py:179
  564.1 14.2 %collective-permute-start.29 = (bf16[128,2048]{1,0:T(8,128)(2,1)S(1)}, bf16[128,2048]{1,0:T(8,128)(2,1)S(1)}, u32[]{:S(2)}, u32[]{:S(2)}) collective-permute-start(bf16[128,2048]{1,0:T(8,128)(2,1)S(1)} %bitcast.688), channel_id=1, source_target_pairs={{0,2},{1,3},{2,0},{3,1},{4,6},{5,7},{6,4},{7,5},{8,10},{9,11},{10,... | collective-permute-start | bytes 1572872 | tf_op jit(solution)/shard_map/ppermute | solution.py:179
  572.2 14.1 %collective-permute-start.39 = (bf16[256,1024]{1,0:T(8,128)(2,1)S(1)}, bf16[256,1024]{1,0:T(8,128)(2,1)S(1)}, u32[]{:S(2)}, u32[]{:S(2)}) collective-permute-start(bf16[256,1024]{1,0:T(8,128)(2,1)S(1)} %bitcast.689), channel_id=1, source_target_pairs={{0,4},{4,0},{8,12},{12,8},{16,20},{20,16},{24,28},{28,24},{1,5},{5... | collective-permute-start | bytes 1572872 | tf_op jit(solution)/shard_map/ppermute | solution.py:179
  576.1 11.2 %collective-permute-start.25 = (bf16[128,1024]{1,0:T(8,128)(2,1)S(1)}, bf16[128,1024]{1,0:T(8,128)(2,1)S(1)}, u32[]{:S(2)}, u32[]{:S(2)}) collective-permute-start(bf16[128,1024]{1,0:T(8,128)(2,1)S(1)} %bitcast.698), channel_id=1, source_target_pairs={{0,2},{1,3},{2,0},{3,1},{4,6},{5,7},{6,4},{7,5},{8,10},{9,11},{10,... | collective-permute-start | bytes 786440 | tf_op jit(solution)/shard_map/ppermute | solution.py:179
  578.3 10.3 %collective-permute-start.35 = (bf16[64,2048]{1,0:T(8,128)(2,1)S(1)}, bf16[64,2048]{1,0:T(8,128)(2,1)S(1)}, u32[]{:S(2)}, u32[]{:S(2)}) collective-permute-start(bf16[64,2048]{1,0:T(8,128)(2,1)S(1)} %bitcast.699), channel_id=1, source_target_pairs={{0,8},{4,12},{8,0},{12,4},{16,24},{20,28},{24,16},{28,20},{1,9},{5... | collective-permute-start | bytes 786440 | tf_op jit(solution)/shard_map/ppermute | solution.py:179
  586.3 7.3 %collective-permute-start.30 = (bf16[64,2048]{1,0:T(8,128)(2,1)S(1)}, bf16[64,2048]{1,0:T(8,128)(2,1)S(1)}, u32[]{:S(2)}, u32[]{:S(2)}) collective-permute-start(bf16[64,2048]{1,0:T(8,128)(2,1)S(1)} %bitcast.700), channel_id=1, source_target_pairs={{0,4},{4,0},{8,12},{12,8},{16,20},{20,16},{24,28},{28,24},{1,5},{5... | collective-permute-start | bytes 786440 | tf_op jit(solution)/shard_map/ppermute | solution.py:179
  587.3 10.4 %collective-permute-start.40 = (bf16[128,1024]{1,0:T(8,128)(2,1)S(1)}, bf16[128,1024]{1,0:T(8,128)(2,1)S(1)}, u32[]{:S(2)}, u32[]{:S(2)}) collective-permute-start(bf16[128,1024]{1,0:T(8,128)(2,1)S(1)} %bitcast.701), channel_id=1, source_target_pairs={{0,8},{4,12},{8,0},{12,4},{16,24},{20,28},{24,16},{28,20},{1,9},{5... | collective-permute-start | bytes 786440 | tf_op jit(solution)/shard_map/ppermute | solution.py:179
  588.5 39.0 %collective-permute-start.26 = (bf16[64,1024]{1,0:T(8,128)(2,1)S(1)}, bf16[64,1024]{1,0:T(8,128)(2,1)}, u32[]{:S(2)}, u32[]{:S(2)}) collective-permute-start(bf16[64,1024]{1,0:T(8,128)(2,1)S(1)} %dynamic-slice_bitcast_fusion.4), channel_id=1, source_target_pairs={{0,16},{4,20},{8,24},{12,28},{16,0},{20,4},{24,8},{28,12},{1,17},{... | collective-permute-start | bytes 393224 | tf_op jit(solution)/shard_map/ppermute | solution.py:179
  593.6 13.7 %collective-permute-start.36 = (bf16[32,2048]{1,0:T(8,128)(2,1)S(1)}, bf16[32,2048]{1,0:T(8,128)(2,1)S(1)}, u32[]{:S(2)}, u32[]{:S(2)}) collective-permute-start(bf16[32,2048]{1,0:T(8,128)(2,1)S(1)} %dynamic-slice_bitcast_fusion.2), channel_id=1, source_target_pairs={{0,16},{4,20},{8,24},{12,28},{16,0},{20,4},{24,8},{28,12},{1,17},{... | collective-permute-start | bytes 393224 | tf_op jit(solution)/shard_map/ppermute | solution.py:179
  597.8 11.8 %collective-permute-start.31 = (bf16[32,2048]{1,0:T(8,128)(2,1)S(1)}, bf16[32,2048]{1,0:T(8,128)(2,1)S(1)}, u32[]{:S(2)}, u32[]{:S(2)}) collective-permute-start(bf16[32,2048]{1,0:T(8,128)(2,1)S(1)} %dynamic-slice_bitcast_fusion.3), channel_id=1, source_target_pairs={{0,16},{4,20},{8,24},{12,28},{16,0},{20,4},{24,8},{28,12},{1,17},{... | collective-permute-start | bytes 393224 | tf_op jit(solution)/shard_map/ppermute | solution.py:179
  607.3 22.3 %collective-permute-start.41 = (bf16[64,1024]{1,0:T(8,128)(2,1)}, bf16[64,1024]{1,0:T(8,128)(2,1)}, u32[]{:S(2)}, u32[]{:S(2)}) collective-permute-start(bf16[64,1024]{1,0:T(8,128)(2,1)} %dynamic-slice_bitcast_fusion.1), channel_id=1, source_target_pairs={{0,16},{4,20},{8,24},{12,28},{16,0},{20,4},{24,8},{28,12},{1,17},{... | collective-permute-start | bytes 393224 | tf_op jit(solution)/shard_map/ppermute | solution.py:179
  620.9 22.4 %collective-permute-start.18 = (bf16[256,1816]{0,1:T(8,128)(2,1)}, bf16[256,1816]{0,1:T(8,128)(2,1)}, u32[]{:S(2)}, u32[]{:S(2)}) collective-permute-start(bf16[256,1816]{0,1:T(8,128)(2,1)} %copy.441), channel_id=1, source_target_pairs={{0,8},{4,12},{8,0},{12,4},{16,24},{20,28},{24,16},{28,20},{1,9},{5... | collective-permute-start | bytes 2789384 | tf_op jit(solution)/shard_map/ppermute | solution.py:179
  624.4 27.8 %collective-permute-start.13 = (bf16[256,2304]{1,0:T(8,128)(2,1)}, bf16[256,2304]{1,0:T(8,128)(2,1)}, u32[]{:S(2)}, u32[]{:S(2)}) collective-permute-start(bf16[256,2304]{1,0:T(8,128)(2,1)} %bitcast.84), channel_id=1, source_target_pairs={{0,4},{4,0},{8,12},{12,8},{16,20},{20,16},{24,28},{28,24},{1,5},{5... | collective-permute-start | bytes 3538952 | tf_op jit(solution)/shard_map/ppermute | solution.py:179
  645.3 11.9 %collective-permute-start.19 = (bf16[128,1816]{1,0:T(8,128)(2,1)S(1)}, bf16[128,1816]{1,0:T(8,128)(2,1)S(1)}, u32[]{:S(2)}, u32[]{:S(2)}) collective-permute-start(bf16[128,1816]{1,0:T(8,128)(2,1)S(1)} %bitcast.692), channel_id=1, source_target_pairs={{0,2},{1,3},{2,0},{3,1},{4,6},{5,7},{6,4},{7,5},{8,10},{9,11},{10,... | collective-permute-start | bytes 1394696 | tf_op jit(solution)/shard_map/ppermute | solution.py:179
  653.8 12.8 %collective-permute-start.14 = (bf16[128,2304]{1,0:T(8,128)(2,1)S(1)}, bf16[128,2304]{1,0:T(8,128)(2,1)S(1)}, u32[]{:S(2)}, u32[]{:S(2)}) collective-permute-start(bf16[128,2304]{1,0:T(8,128)(2,1)S(1)} %bitcast.680), channel_id=1, source_target_pairs={{0,8},{4,12},{8,0},{12,4},{16,24},{20,28},{24,16},{28,20},{1,9},{5... | collective-permute-start | bytes 1769480 | tf_op jit(solution)/shard_map/ppermute | solution.py:179
  657.4 9.7 %collective-permute-start.20 = (bf16[64,1816]{1,0:T(8,128)(2,1)S(1)}, bf16[64,1816]{1,0:T(8,128)(2,1)S(1)}, u32[]{:S(2)}, u32[]{:S(2)}) collective-permute-start(bf16[64,1816]{1,0:T(8,128)(2,1)S(1)} %bitcast.708), channel_id=1, source_target_pairs={{0,4},{4,0},{8,12},{12,8},{16,20},{20,16},{24,28},{28,24},{1,5},{5... | collective-permute-start | bytes 697352 | tf_op jit(solution)/shard_map/ppermute | solution.py:179
  666.9 6.8 collective-permute-start.15
  (139 other events, 1539.3 us)
Sparse Core Ops, SparseCore 0:
  11.5 105.0 all-gather.9
  120.1 77.0 all-gather.7
  255.4 18.1 all-gather.11
  333.0 53.8 reduce-scatter.1
  389.0 36.3 all-gather.13

commit v3 on v2

--- a/solution.py
+++ b/solution.py
@@ -287,10 +287,12 @@
     full_packed = lax.all_gather(
         pack_project(w_project, gains, conv_params), ("batch", "seq"), axis=0, tiled=True
     )
+    pair = jnp.concatenate([w_mixout, w_down], axis=0).astype(jnp.bfloat16)
+    pair, full_packed = lax.optimization_barrier((pair, full_packed))
     full_project = full_packed[:, : w_project.shape[1]]
     full_gains, full_conv = unpack_vectors(full_packed, w_project.shape[1], devices, gains, conv_params)
     full_pair = lax.all_gather(
-        jnp.concatenate([w_mixout, w_down], axis=0).astype(jnp.bfloat16),
+        pair,
         ("batch", "seq"),
         axis=0,
     )

time: 700 us -> 658 us (0.940)
  waiting for transfers between devices: 241 us -> 194 us
    ppermute x45, waiting for transfers between devices: 156 us -> 123 us  [swapped(): return lax.ppermute(value, axis, pairs)]
    all_gather x1, waiting for transfers between devices: 73.6 us -> 50.9 us  [local(): lax.all_gather(pack_project(w_project, gains, conv_params), ('batch', 'se...]
    all_gather x1, waiting for transfers between devices: 0.01 us -> 20 us  [local(): full_pair = lax.all_gather(pair, ('batch', 'seq'), axis=0)]
    all_gather x1, waiting for transfers between devices: 11.2 us -> 0.01 us  [entering(): lax.all_gather(a.astype(kind), axis)]
    dynamic_slice x24 -> x22, local copies, waits for them, and re-layouts: 30.9 us -> 29.2 us  [scatter_rows(): keep = lax.dynamic_index_in_dim(split, place, 1, False).reshape(-1, width)]
    unnamed x277 -> x269, local copies, waits for them, and re-layouts: 24.2 us -> 23.1 us
  transfers between devices with their start and end apart: 52 -> 52, of which waited for: 25 -> 22; matrix products, arithmetic and copies ran while one was open for 35% -> 43% of each run, Pallas kernels for 0% -> 0%
where the time goes in v3:
time: 658 us; the launch traced here: 647 us
  waiting for transfers between devices  194 us (29%)
  local copies, waits for them, and re-layouts  133 us (20%)
  other arithmetic  109 us (17%)
  matrix products  99.8 us (15%)
  starting transfers between devices  78.2 us (12%)
  between operations  16.9 us (3%)
  blocking collectives  14.5 us (2%)
    ppermute x45, waiting for transfers between devices, swapped(): return lax.ppermute(value, axis, pairs)  123 us
    ppermute x45, starting transfers between devices, swapped(): return lax.ppermute(value, axis, pairs)  74.2 us
    all_gather x1, waiting for transfers between devices, local(): lax.all_gather(pack_project(w_project, gains, conv_params), ('batch', 'se...  50.9 us
    dynamic_slice x22, local copies, waits for them, and re-layouts, scatter_rows(): keep = lax.dynamic_index_in_dim(split, place, 1, False).reshape(-1, width)  29.2 us
    dot_general x3, matrix products, mamba_output(): within = jnp.einsum('tsh,shp->thp', mixing, inputs, precision=highest)  25.7 us
    convert_element_type x28, other arithmetic, scatter_rows(): (keep.astype(jnp.float32) + got.astype(jnp.float32)).astype(total.dtype)  25.1 us
    unnamed x269, local copies, waits for them, and re-layouts  23.1 us
    all_gather x1, waiting for transfers between devices, local(): full_pair = lax.all_gather(pair, ('batch', 'seq'), axis=0)  20 us
  transfers between devices with their start and end apart: 52, of which 22 were waited for; matrix products, arithmetic and copies ran while one was open for 43% of the time, Pallas kernels for 0%

profile of v3, /device:TPU:0, one launch (start us, length us, event | category | flops | bytes accessed | tf_op | source)
XLA Modules:
  0.0 646.8 jit_solution(12251412912252050851)
XLA Ops:
  12.0 4.1 collective-permute-start.1
  17.8 4.6 collective-permute-done.1
  22.6 4.1 collective-permute-start.2
  26.7 8.2 %collective-permute-done.6 = bf16[32,2048]{1,0:T(8,128)(2,1)S(1)} collective-permute-done((bf16[32,2048]{1,0:T(8,128)(2,1)S(1)}, bf16[32,2048]{1,0:T(8,128)(2,1)S(1)}, u32[]{:S(2)}, u32[]{:S(2)}) %collective-permute-start.6) | collective-permute-done | bytes 131104 | tf_op jit(solution)/shard_map/ppermute | solution.py:179
  42.3 14.8 %collective-permute-done.3 = bf16[128,2048]{1,0:T(8,128)(2,1)S(1)} collective-permute-done((bf16[128,2048]{1,0:T(8,128)(2,1)S(1)}, bf16[128,2048]{1,0:T(8,128)(2,1)S(1)}, u32[]{:S(2)}, u32[]{:S(2)}) %collective-permute-start.3) | collective-permute-done | bytes 524320 | tf_op jit(solution)/shard_map/ppermute | solution.py:179
  59.6 50.9 %all-gather.9.cloned.1.call-done = bf16[1024,4133]{1,0:T(8,128)(2,1)} async-done(((bf16[32,4133]{1,0:T(8,128)(2,1)}), bf16[1024,4133]{1,0:T(8,128)(2,1)}) %all-gather.9.cloned.1.call-update) | async-done | bytes 8464400 | tf_op jit(solution)/shard_map/all_gather | solution.py:287
  112.7 7.2 %fusion.31 = f32[256,4120]{0,1:T(8,128)S(1)} fusion(bf16[1024,4133]{1,0:T(8,128)(2,1)} %all-gather.9.cloned.1.call-done, bf16[256,1024]{1,0:T(8,128)(2,1)S(1)} %copy-done.26, f32[1024]{0:T(1024)S(1)} %get-tuple-element.701, f32[256]{0:T(256)S(1)} %fusion.190), kind=kOutput, calls=%fused_computation.58 | convolution fusion | flops 2161115136 | bytes 13212672 | tf_op jit(solution)/shard_map/dot_general | solution.py:313
  129.1 5.9 fusion.73
  148.8 19.3 %collective-permute-done.9 = bf16[256,2048]{1,0:T(8,128)(2,1)S(1)} collective-permute-done((bf16[256,2048]{1,0:T(8,128)(2,1)S(1)}, bf16[256,2048]{1,0:T(8,128)(2,1)S(1)}, u32[]{:S(2)}, u32[]{:S(2)}) %collective-permute-start.9) | collective-permute-done | bytes 1048608 | tf_op jit(solution)/shard_map/ppermute | solution.py:179
  184.8 5.2 all-gather.3
  193.2 9.3 %all_gather.31 = bf16[1024,256]{0,1:T(8,128)(2,1)S(1)} all-gather(bf16[256,256]{0,1:T(8,128)(2,1)S(1)} %pad_maximum_fusion.20), channel_id=1, replica_groups=mesh['batch'=8,'seq'=4] {'seq'}, dimensions={0}, use_global_device_ids=true | all-gather | bytes 655360 | tf_op jit(solution)/shard_map/all_gather | solution.py:330
  205.9 3.7 while.67
  216.5 7.0 %fusion.77 = f32[256,24,64]{0,2,1:T(8,128)S(1)} fusion(f32[256,24,64]{0,2,1:T(8,128)S(1)} %bitcast.602, f32[256,24,64]{0,2,1:T(8,128)S(1)} %fusion.166, f32[256,24]{0,1:T(8,128)S(1)} %bitcast_bitcast_fusion, f32[256,256]{1,0:T(8,128)S(1)} %copy-done.71, pred[256,256]{1,0:T(8,128)(4,1)S(1)} %copy-done.97, f32[24]{0:T(128)S(1)} %copy-done.126, ...), kind=kOutput, calls=%fused_computation.155 | convolution fusion | flops 1214644224 | bytes 5120096 | tf_op jit(solution)/shard_map/jvp(tsh,shp->thp)/dot_general | solution.py:143
  228.7 20.0 %all-gather.13.cloned.1.call-done = bf16[4096,1024]{1,0:T(8,128)(2,1)} async-done(((bf16[128,1024]{1,0:T(8,128)(2,1)}), bf16[4096,1024]{1,0:T(8,128)(2,1)}) %all-gather.13.cloned.1.call-update) | async-done | bytes 8388624 | tf_op jit(solution)/shard_map/all_gather | solution.py:294
  248.8 4.4 fusion.218
  267.4 3.4 convolution_convert_fusion.4
  276.6 3.6 convolution_convert_fusion.3
  287.9 8.5 %while.68 = (s32[]{:T(128)}, f32[256,2,4,64]{0,3,2,1:T(8,128)}, bf16[1024,256]{1,0:T(8,128)(2,1)}, s32[]{:T(128)}, bf16[1024,128]{0,1:T(8,128)(2,1)}, /*index=5*...) while((s32[]{:T(128)}, f32[256,2,4,64]{0,3,2,1:T(8,128)}, ...), condition=%wide.region_16.17_spmd.clone, body=%wide.region_15.16_spmd.clone.sunk | while | flops 340460032 | bytes 14110959 | solution.py:490
  298.6 4.3 multiply_reduce_fusion.4
  306.0 4.0 fusion.109
  310.0 7.7 %constant_dynamic-slice_fusion.13 = (bf16[16,1,64,1024]{3,2,1,0:T(8,128)(2,1)}, bf16[16,1,64,1024]{3,2,1,0:T(8,128)(2,1)}, bf16[16,1,64,1024]{3,2,1,0:T(8,128)(2,1)}, bf16[16,1,64,1024]{3,2,1,0:T(8,128)(2,1)}) fusion(bf16[16,2,64,1024]{3,2,1,0:T(8,128)(2,1)} %bitcast.593, s32[]{:T(128)S(6)} %select_n.599, s32[]{:T(128)S(6)} %select_n.600, ...), kind=kLoop, calls=%fused_computation.397 | loop fusion | bytes 16777224 | tf_op jit(solution)/shard_map/jit(dynamic_index_in_dim)/dynamic_slice | solution.py:211
  317.8 8.8 %collective-permute-start.22 = (bf16[1024,1024]{1,0:T(8,128)(2,1)}, bf16[1024,1024]{1,0:T(8,128)(2,1)}, u32[]{:S(2)}, u32[]{:S(2)}) collective-permute-start(bf16[1024,1024]{1,0:T(8,128)(2,1)} %bitcast.110), channel_id=1, source_target_pairs={{0,1},{1,0},{2,3},{3,2},{4,5},{5,4},{6,7},{7,6},{8,9},{9,8},{10,11... | collective-permute-start | bytes 6291464 | tf_op jit(solution)/shard_map/ppermute | solution.py:179
  326.5 3.5 constant_dynamic-slice_fusion.21
  332.3 3.6 fusion.100
  335.9 11.4 %fusion.47 = (f32[256,24]{0,1:T(8,128)}, f32[256,24]{0,1:T(8,128)}, f32[256,256]{1,0:T(8,128)S(1)}) fusion(f32[256,24]{0,1:T(8,128)} %copy-done.82, f32[256,256]{1,0:T(8,128)} %fusion.171, pred[256,256]{1,0:T(8,128)(4,1)} %iota_compare_fusion, f32[24,64,256]{2,1,0:T(8,128)} %bitcast.607, f32[256,24,64]{0,2,1:T(8,128)} %bitcast.601, f32[256,24]{0,1:T(8,128)} %copy-done.78), kind=kOutput, calls=%fused_computation.82 | convolution fusion | flops 1222430720 | bytes 3833856 | tf_op jit(solution)/shard_map/transpose(jvp(tsh,shp->thp))/dot_general | solution.py:143
  350.6 4.9 fusion.96
  358.8 4.4 fusion.132
  372.9 17.8 %collective-permute-start.33 = (bf16[256,2048]{1,0:T(8,128)(2,1)}, bf16[256,2048]{1,0:T(8,128)(2,1)}, u32[]{:S(2)}, u32[]{:S(2)}) collective-permute-start(bf16[256,2048]{1,0:T(8,128)(2,1)} %bitcast.143), channel_id=1, source_target_pairs={{0,2},{1,3},{2,0},{3,1},{4,6},{5,7},{6,4},{7,5},{8,10},{9,11},{10,... | collective-permute-start | bytes 3145736 | tf_op jit(solution)/shard_map/ppermute | solution.py:179
  401.2 5.1 while.69
  412.2 7.3 %multiply_reduce_fusion.6 = (f32[256,24]{0,1:T(8,128)}, f32[256,24]{0,1:T(8,128)}, f32[256,24,64]{0,2,1:T(8,128)}, f32[256,24]{0,1:T(8,128)}) fusion(f32[256,24,64]{0,2,1:T(8,128)S(1)} %fusion.162, f32[256,24,64]{0,2,1:T(8,128)S(1)} %bitcast.604, f32[256,24]{0,1:T(8,128)S(1)} %copy-done.79, f32[256,24,64]{0,2,1:T(8,128)S(1)} %bitcast.608, ...), kind=kOutput, calls=%fused_computation.159 | convolution fusion | flops 1217378304 | bytes 9912416 | tf_op jit(solution)/shard_map/transpose(jvp(tsh,shp->thp))/dot_general | solution.py:143
  424.3 3.9 multiply_reduce_fusion.2
  453.5 5.3 fusion.113
  468.5 6.7 %copy.436 = bf16[1024,2304]{1,0:T(8,128)(2,1)} copy(bf16[1024,2304]{0,1:T(8,128)(2,1)} %slice.285) | data formatting | bytes 9437184 | tf_op jit(solution)/shard_map/slice | solution.py:531
  476.6 4.2 constant_dynamic-slice_fusion.53
  487.5 4.4 slice.286
  491.9 6.0 copy.437
  500.3 4.4 constant_dynamic-slice_fusion.45
  504.7 4.3 copy.438
  525.5 5.2 collective-permute-done.24
  539.1 5.4 collective-permute-done.39
  557.9 7.6 %collective-permute-done.36 = bf16[32,2048]{1,0:T(8,128)(2,1)S(1)} collective-permute-done((bf16[32,2048]{1,0:T(8,128)(2,1)S(1)}, bf16[32,2048]{1,0:T(8,128)(2,1)S(1)}, u32[]{:S(2)}, u32[]{:S(2)}) %collective-permute-start.36) | collective-permute-done | bytes 131104 | tf_op jit(solution)/shard_map/ppermute | solution.py:179
  565.5 5.1 collective-permute-done.31
  572.1 3.9 copy.439
  589.5 11.6 %collective-permute-done.18 = bf16[256,1816]{0,1:T(8,128)(2,1)} collective-permute-done((bf16[256,1816]{0,1:T(8,128)(2,1)}, bf16[256,1816]{0,1:T(8,128)(2,1)}, u32[]{:S(2)}, u32[]{:S(2)}) %collective-permute-start.18) | collective-permute-done | bytes 929824 | tf_op jit(solution)/shard_map/ppermute | solution.py:179
  603.9 6.0 collective-permute-done.13
  614.1 9.4 %collective-permute-done.14 = bf16[128,2304]{1,0:T(8,128)(2,1)S(1)} collective-permute-done((bf16[128,2304]{1,0:T(8,128)(2,1)S(1)}, bf16[128,2304]{1,0:T(8,128)(2,1)S(1)}, u32[]{:S(2)}, u32[]{:S(2)}) %collective-permute-start.14) | collective-permute-done | bytes 589856 | tf_op jit(solution)/shard_map/ppermute | solution.py:179
  626.7 3.8 collective-permute-done.15
  632.6 5.7 collective-permute-done.16
  (649 shorter events, 277.9 us)
Async XLA Ops:
  7.2 103.3 %all-gather.9.cloned.1.call-start = ((), (), s32[]{:S(2)}) async-start(), calls=%async_computation.1 | async-start | bytes 8921088 | tf_op jit(solution)/shard_map/all_gather | solution.py:287
  10.9 203.5 %all-gather.11.cloned.1.call-start = ((), (), s32[]{:S(2)}) async-start(), calls=%async_computation.3 | async-start | bytes 1966080 | tf_op jit(solution)/shard_map/all_gather | solution.py:38
  12.0 10.4 %collective-permute-start.1 = (bf16[32,2048]{1,0:T(8,128)(2,1)S(1)}, bf16[32,2048]{1,0:T(8,128)(2,1)S(1)}, u32[]{:S(2)}, u32[]{:S(2)}) collective-permute-start(bf16[32,2048]{1,0:T(8,128)(2,1)S(1)} %slice.275), channel_id=1, source_target_pairs={{0,16},{4,20},{8,24},{12,28},{16,0},{20,4},{24,8},{28,12},{1,17},{... | collective-permute-start | bytes 393224 | tf_op jit(solution)/shard_map/ppermute | solution.py:179
  22.5 12.4 %collective-permute-start.6 = (bf16[32,2048]{1,0:T(8,128)(2,1)S(1)}, bf16[32,2048]{1,0:T(8,128)(2,1)S(1)}, u32[]{:S(2)}, u32[]{:S(2)}) collective-permute-start(bf16[32,2048]{1,0:T(8,128)(2,1)S(1)} %get-tuple-element.691), channel_id=1, source_target_pairs={{0,16},{4,20},{8,24},{12,28},{16,0},{20,4},{24,8},{28,12},{1,17},{... | collective-permute-start | bytes 393224 | tf_op jit(solution)/shard_map/ppermute | solution.py:179
  22.6 16.9 %collective-permute-start.2 = (bf16[64,2048]{1,0:T(8,128)(2,1)S(1)}, bf16[64,2048]{1,0:T(8,128)(2,1)S(1)}, u32[]{:S(2)}, u32[]{:S(2)}) collective-permute-start(bf16[64,2048]{1,0:T(8,128)(2,1)S(1)} %bitcast.698), channel_id=1, source_target_pairs={{0,8},{4,12},{8,0},{12,4},{16,24},{20,28},{24,16},{28,20},{1,9},{5... | collective-permute-start | bytes 786440 | tf_op jit(solution)/shard_map/ppermute | solution.py:179
  39.6 17.6 %collective-permute-start.3 = (bf16[128,2048]{1,0:T(8,128)(2,1)S(1)}, bf16[128,2048]{1,0:T(8,128)(2,1)S(1)}, u32[]{:S(2)}, u32[]{:S(2)}) collective-permute-start(bf16[128,2048]{1,0:T(8,128)(2,1)S(1)} %bitcast.652), channel_id=1, source_target_pairs={{0,4},{4,0},{8,12},{12,8},{16,20},{20,16},{24,28},{28,24},{1,5},{5... | collective-permute-start | bytes 1572872 | tf_op jit(solution)/shard_map/ppermute | solution.py:179
  42.3 98.6 %collective-permute-start.8 = (bf16[128,2048]{1,0:T(8,128)(2,1)}, bf16[128,2048]{1,0:T(8,128)(2,1)}, u32[]{:S(2)}, u32[]{:S(2)}) collective-permute-start(bf16[128,2048]{1,0:T(8,128)(2,1)} %bitcast.44), channel_id=1, source_target_pairs={{0,8},{4,12},{8,0},{12,4},{16,24},{20,28},{24,16},{28,20},{1,9},{5... | collective-permute-start | bytes 1572872 | tf_op jit(solution)/shard_map/ppermute | solution.py:179
  58.4 85.7 %collective-permute-start.4 = (bf16[256,2048]{1,0:T(8,128)(2,1)}, bf16[256,2048]{1,0:T(8,128)(2,1)}, u32[]{:S(2)}, u32[]{:S(2)}) collective-permute-start(bf16[256,2048]{1,0:T(8,128)(2,1)} %bitcast.32), channel_id=1, source_target_pairs={{0,2},{1,3},{2,0},{3,1},{4,6},{5,7},{6,4},{7,5},{8,10},{9,11},{10,... | collective-permute-start | bytes 3145736 | tf_op jit(solution)/shard_map/ppermute | solution.py:179
  122.4 6.7 %collective-permute-start = (f32[3,1792]{1,0:T(4,128)S(1)}, f32[3,1792]{1,0:T(4,128)S(1)}, u32[]{:S(2)}, u32[]{:S(2)}) collective-permute-start(f32[3,1792]{1,0:T(4,128)S(1)} %copy.401), channel_id=1, source_target_pairs={{0,1},{1,2},{2,3},{4,5},{5,6},{6,7},{8,9},{9,10},{10,11},{12,13},{... | collective-permute-start | bytes 64520 | tf_op jit(solution)/shard_map/ppermute | solution.py:32
  140.7 108.1 %all-gather.13.cloned.1.call-start = ((), (), s32[]{:S(2)}) async-start(), calls=%async_computation.4 | async-start | bytes 8650752 | tf_op jit(solution)/shard_map/all_gather | solution.py:294
  142.4 25.7 %collective-permute-start.9 = (bf16[256,2048]{1,0:T(8,128)(2,1)S(1)}, bf16[256,2048]{1,0:T(8,128)(2,1)S(1)}, u32[]{:S(2)}, u32[]{:S(2)}) collective-permute-start(bf16[256,2048]{1,0:T(8,128)(2,1)S(1)} %bitcast.629), channel_id=1, source_target_pairs={{0,4},{4,0},{8,12},{12,8},{16,20},{20,16},{24,28},{28,24},{1,5},{5... | collective-permute-start | bytes 3145736 | tf_op jit(solution)/shard_map/ppermute | solution.py:179
  147.6 23.7 %collective-permute-start.5 = (bf16[512,2048]{1,0:T(8,128)(2,1)}, bf16[512,2048]{1,0:T(8,128)(2,1)}, u32[]{:S(2)}, u32[]{:S(2)}) collective-permute-start(bf16[512,2048]{1,0:T(8,128)(2,1)} %bitcast.35), channel_id=1, source_target_pairs={{0,1},{1,0},{2,3},{3,2},{4,5},{5,4},{6,7},{7,6},{8,9},{9,8},{10,11... | collective-permute-start | bytes 6291464 | tf_op jit(solution)/shard_map/ppermute | solution.py:179
  170.2 185.3 %reduce-scatter.2.cloned.1.call-start = ((), (), s32[]{:S(2)}) async-start(), calls=%async_computation.2 | async-start | bytes 655360 | tf_op jit(solution)/shard_map/reduce_scatter | solution.py:499
  298.5 102.7 %all-gather.15.cloned.1.call-start = ((), (), s32[]{:S(2)}) async-start(), calls=%async_computation.5 | async-start | bytes 1966080 | tf_op jit(solution)/shard_map/all_gather | solution.py:58
  317.8 45.4 %collective-permute-start.22 = (bf16[1024,1024]{1,0:T(8,128)(2,1)}, bf16[1024,1024]{1,0:T(8,128)(2,1)}, u32[]{:S(2)}, u32[]{:S(2)}) collective-permute-start(bf16[1024,1024]{1,0:T(8,128)(2,1)} %bitcast.110), channel_id=1, source_target_pairs={{0,1},{1,0},{2,3},{3,2},{4,5},{5,4},{6,7},{7,6},{8,9},{9,8},{10,11... | collective-permute-start | bytes 6291464 | tf_op jit(solution)/shard_map/ppermute | solution.py:179
  330.1 38.8 %collective-permute-start.32 = (bf16[512,2048]{1,0:T(8,128)(2,1)}, bf16[512,2048]{1,0:T(8,128)(2,1)}, u32[]{:S(2)}, u32[]{:S(2)}) collective-permute-start(bf16[512,2048]{1,0:T(8,128)(2,1)} %bitcast.140), channel_id=1, source_target_pairs={{0,1},{1,0},{2,3},{3,2},{4,5},{5,4},{6,7},{7,6},{8,9},{9,8},{10,11... | collective-permute-start | bytes 6291464 | tf_op jit(solution)/shard_map/ppermute | solution.py:179
  330.4 60.4 %collective-permute-start.27 = (bf16[512,2048]{1,0:T(8,128)(2,1)}, bf16[512,2048]{1,0:T(8,128)(2,1)}, u32[]{:S(2)}, u32[]{:S(2)}) collective-permute-start(bf16[512,2048]{1,0:T(8,128)(2,1)} %bitcast.125), channel_id=1, source_target_pairs={{0,1},{1,0},{2,3},{3,2},{4,5},{5,4},{6,7},{7,6},{8,9},{9,8},{10,11... | collective-permute-start | bytes 6291464 | tf_op jit(solution)/shard_map/ppermute | solution.py:179
  330.6 65.5 %collective-permute-start.37 = (bf16[1024,1024]{1,0:T(8,128)(2,1)}, bf16[1024,1024]{1,0:T(8,128)(2,1)}, u32[]{:S(2)}, u32[]{:S(2)}) collective-permute-start(bf16[1024,1024]{1,0:T(8,128)(2,1)} %bitcast.155), channel_id=1, source_target_pairs={{0,1},{1,0},{2,3},{3,2},{4,5},{5,4},{6,7},{7,6},{8,9},{9,8},{10,11... | collective-permute-start | bytes 6291464 | tf_op jit(solution)/shard_map/ppermute | solution.py:179
  367.4 147.1 %collective-permute-start.23 = (bf16[512,1024]{1,0:T(8,128)(2,1)}, bf16[512,1024]{1,0:T(8,128)(2,1)}, u32[]{:S(2)}, u32[]{:S(2)}) collective-permute-start(bf16[512,1024]{1,0:T(8,128)(2,1)} %bitcast.113), channel_id=1, source_target_pairs={{0,4},{4,0},{8,12},{12,8},{16,20},{20,16},{24,28},{28,24},{1,5},{5... | collective-permute-start | bytes 3145736 | tf_op jit(solution)/shard_map/ppermute | solution.py:179
  372.9 143.9 %collective-permute-start.33 = (bf16[256,2048]{1,0:T(8,128)(2,1)}, bf16[256,2048]{1,0:T(8,128)(2,1)}, u32[]{:S(2)}, u32[]{:S(2)}) collective-permute-start(bf16[256,2048]{1,0:T(8,128)(2,1)} %bitcast.143), channel_id=1, source_target_pairs={{0,2},{1,3},{2,0},{3,1},{4,6},{5,7},{6,4},{7,5},{8,10},{9,11},{10,... | collective-permute-start | bytes 3145736 | tf_op jit(solution)/shard_map/ppermute | solution.py:179
  394.6 125.0 %collective-permute-start.28 = (bf16[256,2048]{1,0:T(8,128)(2,1)}, bf16[256,2048]{1,0:T(8,128)(2,1)}, u32[]{:S(2)}, u32[]{:S(2)}) collective-permute-start(bf16[256,2048]{1,0:T(8,128)(2,1)} %bitcast.128), channel_id=1, source_target_pairs={{0,8},{4,12},{8,0},{12,4},{16,24},{20,28},{24,16},{28,20},{1,9},{5... | collective-permute-start | bytes 3145736 | tf_op jit(solution)/shard_map/ppermute | solution.py:179
  400.3 122.6 %collective-permute-start.38 = (bf16[512,1024]{1,0:T(8,128)(2,1)}, bf16[512,1024]{1,0:T(8,128)(2,1)}, u32[]{:S(2)}, u32[]{:S(2)}) collective-permute-start(bf16[512,1024]{1,0:T(8,128)(2,1)} %bitcast.158), channel_id=1, source_target_pairs={{0,2},{1,3},{2,0},{3,1},{4,6},{5,7},{6,4},{7,5},{8,10},{9,11},{10,... | collective-permute-start | bytes 3145736 | tf_op jit(solution)/shard_map/ppermute | solution.py:179
  433.7 17.8 %collective-permute-start.11 = (f32[3,1792]{1,0:T(4,128)}, f32[3,1792]{1,0:T(4,128)S(1)}, u32[]{:S(2)}, u32[]{:S(2)}) collective-permute-start(f32[3,1792]{1,0:T(4,128)} %pad_add_fusion.2), channel_id=1, source_target_pairs={{1,0},{2,1},{3,2},{5,4},{6,5},{7,6},{9,8},{10,9},{11,10},{13,12},{... | collective-permute-start | bytes 64520 | tf_op jit(solution)/shard_map/ppermute | solution.py:32
  458.9 16.3 %collective-permute-start.42 = (f32[104,128]{1,0:T(8,128)S(1)}, f32[104,128]{1,0:T(8,128)S(1)}, u32[]{:S(2)}, u32[]{:S(2)}) collective-permute-start(f32[104,128]{1,0:T(8,128)S(1)} %pad_bitcast_fusion), channel_id=1, source_target_pairs={{0,1},{1,0},{2,3},{3,2},{4,5},{5,4},{6,7},{7,6},{8,9},{9,8},{10,11... | collective-permute-start | bytes 159752 | tf_op jit(solution)/shard_map/ppermute | solution.py:179
  485.0 12.9 %collective-permute-start.45 = (f32[104,128]{1,0:T(8,128)S(1)}, f32[104,128]{1,0:T(8,128)}, u32[]{:S(2)}, u32[]{:S(2)}) collective-permute-start(f32[104,128]{1,0:T(8,128)S(1)} %add.784), channel_id=1, source_target_pairs={{0,8},{4,12},{8,0},{12,4},{16,24},{20,28},{24,16},{28,20},{1,9},{5... | collective-permute-start | bytes 159752 | tf_op jit(solution)/shard_map/ppermute | solution.py:179
  498.7 10.2 %collective-permute-start.46 = (f32[104,128]{1,0:T(8,128)S(1)}, f32[104,128]{1,0:T(8,128)S(1)}, u32[]{:S(2)}, u32[]{:S(2)}) collective-permute-start(f32[104,128]{1,0:T(8,128)S(1)} %add.785), channel_id=1, source_target_pairs={{0,16},{4,20},{8,24},{12,28},{16,0},{20,4},{24,8},{28,12},{1,17},{... | collective-permute-start | bytes 159752 | tf_op jit(solution)/shard_map/ppermute | solution.py:179
  509.6 62.6 %collective-permute-start.17 = (bf16[512,1816]{0,1:T(8,128)(2,1)}, bf16[512,1816]{0,1:T(8,128)(2,1)}, u32[]{:S(2)}, u32[]{:S(2)}) collective-permute-start(bf16[512,1816]{0,1:T(8,128)(2,1)} %copy.438), channel_id=1, source_target_pairs={{0,1},{1,0},{2,3},{3,2},{4,5},{5,4},{6,7},{7,6},{8,9},{9,8},{10,11... | collective-permute-start | bytes 5578760 | tf_op jit(solution)/shard_map/ppermute | solution.py:179
  514.5 67.5 %collective-permute-start.12 = (bf16[512,2304]{1,0:T(8,128)(2,1)}, bf16[512,2304]{1,0:T(8,128)(2,1)}, u32[]{:S(2)}, u32[]{:S(2)}) collective-permute-start(bf16[512,2304]{1,0:T(8,128)(2,1)} %bitcast.646), channel_id=1, source_target_pairs={{0,1},{1,0},{2,3},{3,2},{4,5},{5,4},{6,7},{7,6},{8,9},{9,8},{10,11... | collective-permute-start | bytes 7077896 | tf_op jit(solution)/shard_map/ppermute | solution.py:179
  516.8 13.9 %collective-permute-start.24 = (bf16[256,1024]{1,0:T(8,128)(2,1)S(1)}, bf16[256,1024]{1,0:T(8,128)(2,1)S(1)}, u32[]{:S(2)}, u32[]{:S(2)}) collective-permute-start(bf16[256,1024]{1,0:T(8,128)(2,1)S(1)} %bitcast.680), channel_id=1, source_target_pairs={{0,8},{4,12},{8,0},{12,4},{16,24},{20,28},{24,16},{28,20},{1,9},{5... | collective-permute-start | bytes 1572872 | tf_op jit(solution)/shard_map/ppermute | solution.py:179
  519.6 14.3 %collective-permute-start.34 = (bf16[128,2048]{1,0:T(8,128)(2,1)S(1)}, bf16[128,2048]{1,0:T(8,128)(2,1)S(1)}, u32[]{:S(2)}, u32[]{:S(2)}) collective-permute-start(bf16[128,2048]{1,0:T(8,128)(2,1)S(1)} %bitcast.681), channel_id=1, source_target_pairs={{0,4},{4,0},{8,12},{12,8},{16,20},{20,16},{24,28},{28,24},{1,5},{5... | collective-permute-start | bytes 1572872 | tf_op jit(solution)/shard_map/ppermute | solution.py:179
  522.9 14.8 %collective-permute-start.29 = (bf16[128,2048]{1,0:T(8,128)(2,1)S(1)}, bf16[128,2048]{1,0:T(8,128)(2,1)S(1)}, u32[]{:S(2)}, u32[]{:S(2)}) collective-permute-start(bf16[128,2048]{1,0:T(8,128)(2,1)S(1)} %bitcast.682), channel_id=1, source_target_pairs={{0,2},{1,3},{2,0},{3,1},{4,6},{5,7},{6,4},{7,5},{8,10},{9,11},{10,... | collective-permute-start | bytes 1572872 | tf_op jit(solution)/shard_map/ppermute | solution.py:179
  530.8 13.7 %collective-permute-start.39 = (bf16[256,1024]{1,0:T(8,128)(2,1)S(1)}, bf16[256,1024]{1,0:T(8,128)(2,1)S(1)}, u32[]{:S(2)}, u32[]{:S(2)}) collective-permute-start(bf16[256,1024]{1,0:T(8,128)(2,1)S(1)} %bitcast.683), channel_id=1, source_target_pairs={{0,4},{4,0},{8,12},{12,8},{16,20},{20,16},{24,28},{28,24},{1,5},{5... | collective-permute-start | bytes 1572872 | tf_op jit(solution)/shard_map/ppermute | solution.py:179
  534.0 12.2 %collective-permute-start.25 = (bf16[128,1024]{1,0:T(8,128)(2,1)S(1)}, bf16[128,1024]{1,0:T(8,128)(2,1)S(1)}, u32[]{:S(2)}, u32[]{:S(2)}) collective-permute-start(bf16[128,1024]{1,0:T(8,128)(2,1)S(1)} %bitcast.692), channel_id=1, source_target_pairs={{0,2},{1,3},{2,0},{3,1},{4,6},{5,7},{6,4},{7,5},{8,10},{9,11},{10,... | collective-permute-start | bytes 786440 | tf_op jit(solution)/shard_map/ppermute | solution.py:179
  537.8 9.8 %collective-permute-start.35 = (bf16[64,2048]{1,0:T(8,128)(2,1)S(1)}, bf16[64,2048]{1,0:T(8,128)(2,1)S(1)}, u32[]{:S(2)}, u32[]{:S(2)}) collective-permute-start(bf16[64,2048]{1,0:T(8,128)(2,1)S(1)} %bitcast.693), channel_id=1, source_target_pairs={{0,8},{4,12},{8,0},{12,4},{16,24},{20,28},{24,16},{28,20},{1,9},{5... | collective-permute-start | bytes 786440 | tf_op jit(solution)/shard_map/ppermute | solution.py:179
  544.5 7.2 %collective-permute-start.30 = (bf16[64,2048]{1,0:T(8,128)(2,1)S(1)}, bf16[64,2048]{1,0:T(8,128)(2,1)S(1)}, u32[]{:S(2)}, u32[]{:S(2)}) collective-permute-start(bf16[64,2048]{1,0:T(8,128)(2,1)S(1)} %bitcast.694), channel_id=1, source_target_pairs={{0,4},{4,0},{8,12},{12,8},{16,20},{20,16},{24,28},{28,24},{1,5},{5... | collective-permute-start | bytes 786440 | tf_op jit(solution)/shard_map/ppermute | solution.py:179
  546.2 10.8 %collective-permute-start.40 = (bf16[128,1024]{1,0:T(8,128)(2,1)S(1)}, bf16[128,1024]{1,0:T(8,128)(2,1)S(1)}, u32[]{:S(2)}, u32[]{:S(2)}) collective-permute-start(bf16[128,1024]{1,0:T(8,128)(2,1)S(1)} %bitcast.695), channel_id=1, source_target_pairs={{0,8},{4,12},{8,0},{12,4},{16,24},{20,28},{24,16},{28,20},{1,9},{5... | collective-permute-start | bytes 786440 | tf_op jit(solution)/shard_map/ppermute | solution.py:179
  547.5 38.0 %collective-permute-start.26 = (bf16[64,1024]{1,0:T(8,128)(2,1)S(1)}, bf16[64,1024]{1,0:T(8,128)(2,1)}, u32[]{:S(2)}, u32[]{:S(2)}) collective-permute-start(bf16[64,1024]{1,0:T(8,128)(2,1)S(1)} %dynamic-slice_bitcast_fusion.4), channel_id=1, source_target_pairs={{0,16},{4,20},{8,24},{12,28},{16,0},{20,4},{24,8},{28,12},{1,17},{... | collective-permute-start | bytes 393224 | tf_op jit(solution)/shard_map/ppermute | solution.py:179
  551.7 13.8 %collective-permute-start.36 = (bf16[32,2048]{1,0:T(8,128)(2,1)S(1)}, bf16[32,2048]{1,0:T(8,128)(2,1)S(1)}, u32[]{:S(2)}, u32[]{:S(2)}) collective-permute-start(bf16[32,2048]{1,0:T(8,128)(2,1)S(1)} %dynamic-slice_bitcast_fusion.2), channel_id=1, source_target_pairs={{0,16},{4,20},{8,24},{12,28},{16,0},{20,4},{24,8},{28,12},{1,17},{... | collective-permute-start | bytes 393224 | tf_op jit(solution)/shard_map/ppermute | solution.py:179
  556.9 13.7 %collective-permute-start.31 = (bf16[32,2048]{1,0:T(8,128)(2,1)S(1)}, bf16[32,2048]{1,0:T(8,128)(2,1)S(1)}, u32[]{:S(2)}, u32[]{:S(2)}) collective-permute-start(bf16[32,2048]{1,0:T(8,128)(2,1)S(1)} %dynamic-slice_bitcast_fusion.3), channel_id=1, source_target_pairs={{0,16},{4,20},{8,24},{12,28},{16,0},{20,4},{24,8},{28,12},{1,17},{... | collective-permute-start | bytes 393224 | tf_op jit(solution)/shard_map/ppermute | solution.py:179
  565.5 22.1 %collective-permute-start.41 = (bf16[64,1024]{1,0:T(8,128)(2,1)}, bf16[64,1024]{1,0:T(8,128)(2,1)}, u32[]{:S(2)}, u32[]{:S(2)}) collective-permute-start(bf16[64,1024]{1,0:T(8,128)(2,1)} %dynamic-slice_bitcast_fusion.1), channel_id=1, source_target_pairs={{0,16},{4,20},{8,24},{12,28},{16,0},{20,4},{24,8},{28,12},{1,17},{... | collective-permute-start | bytes 393224 | tf_op jit(solution)/shard_map/ppermute | solution.py:179
  582.1 19.0 %collective-permute-start.18 = (bf16[256,1816]{0,1:T(8,128)(2,1)}, bf16[256,1816]{0,1:T(8,128)(2,1)}, u32[]{:S(2)}, u32[]{:S(2)}) collective-permute-start(bf16[256,1816]{0,1:T(8,128)(2,1)} %copy.441), channel_id=1, source_target_pairs={{0,8},{4,12},{8,0},{12,4},{16,24},{20,28},{24,16},{28,20},{1,9},{5... | collective-permute-start | bytes 2789384 | tf_op jit(solution)/shard_map/ppermute | solution.py:179
  585.6 24.4 %collective-permute-start.13 = (bf16[256,2304]{1,0:T(8,128)(2,1)}, bf16[256,2304]{1,0:T(8,128)(2,1)}, u32[]{:S(2)}, u32[]{:S(2)}) collective-permute-start(bf16[256,2304]{1,0:T(8,128)(2,1)} %bitcast.83), channel_id=1, source_target_pairs={{0,4},{4,0},{8,12},{12,8},{16,20},{20,16},{24,28},{28,24},{1,5},{5... | collective-permute-start | bytes 3538952 | tf_op jit(solution)/shard_map/ppermute | solution.py:179
  603.0 10.4 %collective-permute-start.19 = (bf16[128,1816]{1,0:T(8,128)(2,1)S(1)}, bf16[128,1816]{1,0:T(8,128)(2,1)S(1)}, u32[]{:S(2)}, u32[]{:S(2)}) collective-permute-start(bf16[128,1816]{1,0:T(8,128)(2,1)S(1)} %bitcast.686), channel_id=1, source_target_pairs={{0,2},{1,3},{2,0},{3,1},{4,6},{5,7},{6,4},{7,5},{8,10},{9,11},{10,... | collective-permute-start | bytes 1394696 | tf_op jit(solution)/shard_map/ppermute | solution.py:179
  611.6 11.9 %collective-permute-start.14 = (bf16[128,2304]{1,0:T(8,128)(2,1)S(1)}, bf16[128,2304]{1,0:T(8,128)(2,1)S(1)}, u32[]{:S(2)}, u32[]{:S(2)}) collective-permute-start(bf16[128,2304]{1,0:T(8,128)(2,1)S(1)} %bitcast.676), channel_id=1, source_target_pairs={{0,8},{4,12},{8,0},{12,4},{16,24},{20,28},{24,16},{28,20},{1,9},{5... | collective-permute-start | bytes 1769480 | tf_op jit(solution)/shard_map/ppermute | solution.py:179
  613.6 11.0 %collective-permute-start.20 = (bf16[64,1816]{1,0:T(8,128)(2,1)S(1)}, bf16[64,1816]{1,0:T(8,128)(2,1)S(1)}, u32[]{:S(2)}, u32[]{:S(2)}) collective-permute-start(bf16[64,1816]{1,0:T(8,128)(2,1)S(1)} %bitcast.702), channel_id=1, source_target_pairs={{0,4},{4,0},{8,12},{12,8},{16,20},{20,16},{24,28},{28,24},{1,5},{5... | collective-permute-start | bytes 697352 | tf_op jit(solution)/shard_map/ppermute | solution.py:179
  623.7 6.8 %collective-permute-start.15 = (bf16[64,2304]{1,0:T(8,128)(2,1)S(1)}, bf16[64,2304]{1,0:T(8,128)(2,1)S(1)}, u32[]{:S(2)}, u32[]{:S(2)}) collective-permute-start(bf16[64,2304]{1,0:T(8,128)(2,1)S(1)} %bitcast.691), channel_id=1, source_target_pairs={{0,2},{1,3},{2,0},{3,1},{4,6},{5,7},{6,4},{7,5},{8,10},{9,11},{10,... | collective-permute-start | bytes 884744 | tf_op jit(solution)/shard_map/ppermute | solution.py:179
  624.7 7.9 %collective-permute-start.21 = (bf16[32,1816]{1,0:T(8,128)(2,1)S(1)}, bf16[32,1816]{1,0:T(8,128)(2,1)S(1)}, u32[]{:S(2)}, u32[]{:S(2)}) collective-permute-start(bf16[32,1816]{1,0:T(8,128)(2,1)S(1)} %dynamic-slice_bitcast_fusion.5), channel_id=1, source_target_pairs={{0,16},{4,20},{8,24},{12,28},{16,0},{20,4},{24,8},{28,12},{1,17},{... | collective-permute-start | bytes 348680 | tf_op jit(solution)/shard_map/ppermute | solution.py:179
  630.6 7.7 %collective-permute-start.16 = (bf16[32,2304]{1,0:T(8,128)(2,1)S(1)}, bf16[32,2304]{1,0:T(8,128)(2,1)S(1)}, u32[]{:S(2)}, u32[]{:S(2)}) collective-permute-start(bf16[32,2304]{1,0:T(8,128)(2,1)S(1)} %dynamic-slice_bitcast_fusion), channel_id=1, source_target_pairs={{0,16},{4,20},{8,24},{12,28},{16,0},{20,4},{24,8},{28,12},{1,17},{... | collective-permute-start | bytes 442376 | tf_op jit(solution)/shard_map/ppermute | solution.py:179
  (137 other events, 1701.5 us)
Sparse Core Ops, SparseCore 0:
  11.5 98.9 all-gather.8
  140.8 19.8 all-gather.10
  170.4 78.3 all-gather.12
  298.6 47.5 reduce-scatter.1
  348.2 34.5 all-gather.14
